TPU v7x, 512 devices: a whole 4x4x16 slice. The times are simulated.
512 devices in a mesh: row: 16 (over x, z_lo), col: 32 (over z_hi, y, core).
Axes of the slice: x: 4, y: 4, z: 16 (z_hi: 4, z_lo: 4; z = z_hi * 4 + z_lo), core: 2. Of those that a mesh axis runs over, the one named last changes fastest.
Arguments:
- layer_input: bfloat16 [2048, 8192], P('row', 'col'), may hold values from -6 to 6
- rank_gate: bfloat16 [2048, 3072], P('col', 'row'), may hold values from -6 to 6
- rank_up: bfloat16 [2048, 3072], P('col', 'row'), may hold values from -6 to 6
- gate_pre: bfloat16 [2048, 29568], P('row', 'col'), may hold values from -12 to 12
- up_pre: bfloat16 [2048, 29568], P('row', 'col'), may hold values from -6 to 6
- hidden_grad: bfloat16 [2048, 29568], P('row', 'col'), may hold values from -0.59765625 to 0.59765625
- gate_inner: bfloat16 [8192, 3072], P('col', 'row'), may hold values from -0.0625 to 0.0625
- gate_outer: bfloat16 [3072, 29568], P('row', 'col'), may hold values from -0.109375 to 0.109375
- up_inner: bfloat16 [8192, 3072], P('col', 'row'), may hold values from -0.0625 to 0.0625
- up_outer: bfloat16 [3072, 29568], P('row', 'col'), may hold values from -0.109375 to 0.109375
Outputs:
- gate_inner_grad: float32 [8192, 3072], P('col', 'row')
- gate_outer_grad: float32 [3072, 29568], P('row', 'col')
- up_inner_grad: float32 [8192, 3072], P('col', 'row')
- up_outer_grad: float32 [3072, 29568], P('row', 'col')
- input_grad: bfloat16 [2048, 8192], P('row', 'col')
All inputs are finite; a program needn't handle non-finite values.
Results may differ from a plain program's by a relative error of at most 0.03.
Values may be sent and summed in bfloat16 or wider, within the bound.
No kernel may reach another device: no remote copies, remote signals or barrier semaphores. Data moves between devices by JAX's collectives and lax.ppermute only.
A program may use at most 64 MiB of HBM per device.

v0:
```python
import jax
import jax.numpy as jnp
from jax import lax
from jax.sharding import PartitionSpec as P


def swiglu_back(gate_pre, up_pre, hidden_grad):
    gate_val = gate_pre.astype(jnp.float32)
    up_val = up_pre.astype(jnp.float32)
    grad_val = hidden_grad.astype(jnp.float32)
    logistic = jax.nn.sigmoid(gate_val)
    gate_grad = (grad_val * up_val * logistic * (1.0 + gate_val * (1.0 - logistic))).astype(
        jnp.bfloat16
    )
    up_grad = (grad_val * gate_val * logistic).astype(jnp.bfloat16)
    return (gate_grad, up_grad)


def branch_step(piece, rank_whole, outer_tile):
    outer_grad = jnp.einsum("tr,tf->rf", rank_whole, piece, preferred_element_type=jnp.float32)
    product = jnp.einsum("tf,rf->tr", piece, outer_tile, preferred_element_type=jnp.float32)
    return (outer_grad, product)


def on_device(
    layer_input,
    rank_gate,
    rank_up,
    gate_pre,
    up_pre,
    hidden_grad,
    gate_inner,
    gate_outer,
    up_inner,
    up_outer,
):
    gate_grad, up_grad = swiglu_back(gate_pre, up_pre, hidden_grad)
    gate_whole, up_whole = (
        lax.all_gather(rank_gate, "col", axis=0, tiled=True),
        lax.all_gather(rank_up, "col", axis=0, tiled=True),
    )
    gate_state = branch_step(
        lax.all_gather(gate_grad, "row", axis=0, tiled=True), gate_whole, gate_outer
    )
    up_state = branch_step(lax.all_gather(up_grad, "row", axis=0, tiled=True), up_whole, up_outer)
    gate_outer_grad = gate_state[0]
    gate_part = gate_state[1]
    up_outer_grad = up_state[0]
    up_part = up_state[1]
    gate_share, up_share = (
        lax.psum_scatter(
            gate_part.astype(jnp.bfloat16), "col", scatter_dimension=0, tiled=True
        ).astype(jnp.float32),
        lax.psum_scatter(
            up_part.astype(jnp.bfloat16), "col", scatter_dimension=0, tiled=True
        ).astype(jnp.float32),
    )
    rank_gate_grad, rank_up_grad = (
        lax.all_gather(gate_share.astype(jnp.bfloat16), "col", axis=0, tiled=True),
        lax.all_gather(up_share.astype(jnp.bfloat16), "col", axis=0, tiled=True),
    )
    piece = lax.all_gather(layer_input, "row", axis=0, tiled=True)
    gate_rows = rank_gate_grad
    up_rows = rank_up_grad
    gate_acc = jnp.einsum("td,tr->dr", piece, gate_rows, preferred_element_type=jnp.float32)
    up_acc = jnp.einsum("td,tr->dr", piece, up_rows, preferred_element_type=jnp.float32)
    gate_rows = rank_gate_grad
    up_rows = rank_up_grad
    first = jnp.einsum("tr,dr->td", gate_rows, gate_inner, preferred_element_type=jnp.float32)
    second = jnp.einsum("tr,dr->td", up_rows, up_inner, preferred_element_type=jnp.float32)
    input_grad = lax.psum_scatter(
        (first + second).astype(jnp.bfloat16), "row", scatter_dimension=0, tiled=True
    )
    return (gate_acc, gate_outer_grad, up_acc, up_outer_grad, input_grad)


def solution(mesh):
    return jax.shard_map(
        on_device,
        mesh=mesh,
        in_specs=(
            P("row", "col"),
            P("col", "row"),
            P("col", "row"),
            P("row", "col"),
            P("row", "col"),
            P("row", "col"),
            P("col", "row"),
            P("row", "col"),
            P("col", "row"),
            P("row", "col"),
        ),
        out_specs=(
            P("col", "row"),
            P("row", "col"),
            P("col", "row"),
            P("row", "col"),
            P("row", "col"),
        ),
        check_vma=False,
    )
```

profile of v0, /device:TPU:65, one launch (start us, length us, event | category | flops | bytes accessed | tf_op | source)
XLA Modules:
  0.0 668.4 jit_solution(9668954000799649682)
XLA Ops:
  7.2 2.2 fusion.9
  9.5 0.0 all-gather.8.cloned.1.call-start
  9.5 0.7 all-gather.8.cloned.1.call-update
  10.3 0.0 reduce-scatter.4.cloned.1.call-start
  10.3 107.4 %all-gather.4.cloned.1.call-done = bf16[2048,924]{0,1:T(8,128)(2,1)} async-done(((bf16[128,924]{0,1:T(8,128)(2,1)}), bf16[2048,924]{0,1:T(8,128)(2,1)}) %all-gather.4.cloned.1.call-update) | async-done | bytes 3784720 | tf_op jit(solution)/shard_map/all_gather | solution.py:43
  117.7 4.5 convolution_convert_fusion.1
  122.3 0.0 reduce-scatter.6.cloned.1.call-start
  122.3 109.4 %all-gather.8.cloned.1.call-done = bf16[2048,924]{0,1:T(8,128)(2,1)} async-done(((bf16[128,924]{0,1:T(8,128)(2,1)}), bf16[2048,924]{0,1:T(8,128)(2,1)}) %all-gather.8.cloned.1.call-update) | async-done | bytes 3784720 | tf_op jit(solution)/shard_map/all_gather | solution.py:45
  231.7 4.4 convolution_convert_fusion
  236.2 0.0 all-gather.6.cloned.1.call-start
  236.2 0.5 all-gather.6.cloned.1.call-update
  236.8 0.0 reduce-scatter.8.cloned.1.call-start
  236.8 117.1 %reduce-scatter.4.cloned.1.call-done = bf16[64,192]{1,0:T(8,128)(2,1)} async-done(((bf16[2048,192]{1,0:T(8,128)(2,1)}), bf16[64,192]{1,0:T(8,128)(2,1)}) %reduce-scatter.4.cloned.1.call-update) | async-done | bytes 24592 | tf_op jit(solution)/shard_map/reduce_scatter | solution.py:51
  353.9 61.0 %all_gather.22 = bf16[2048,192]{1,0:T(8,128)(2,1)S(1)} all-gather(bf16[64,192]{1,0:T(8,128)(2,1)} %reduce-scatter.4.cloned.1.call-done), channel_id=1, replica_groups=mesh['row'=16,'col'=32] {'col'}, dimensions={0}, use_global_device_ids=true | all-gather | bytes 811008 | tf_op jit(solution)/shard_map/all_gather | solution.py:59
  414.9 1.8 fusion.10
  416.8 49.7 %reduce-scatter.6.cloned.1.call-done = bf16[64,192]{1,0:T(8,128)(2,1)} async-done(((bf16[2048,192]{1,0:T(8,128)(2,1)}), bf16[64,192]{1,0:T(8,128)(2,1)}) %reduce-scatter.6.cloned.1.call-update) | async-done | bytes 24592 | tf_op jit(solution)/shard_map/reduce_scatter | solution.py:54
  466.5 68.2 %all_gather.26 = bf16[2048,192]{1,0:T(8,128)(2,1)S(1)} all-gather(bf16[64,192]{1,0:T(8,128)(2,1)} %reduce-scatter.6.cloned.1.call-done), channel_id=1, replica_groups=mesh['row'=16,'col'=32] {'col'}, dimensions={0}, use_global_device_ids=true | all-gather | bytes 811008 | tf_op jit(solution)/shard_map/all_gather | solution.py:60
  534.7 3.0 fusion
  537.7 54.8 %all_gather.24 = bf16[2048,192]{1,0:T(8,128)(2,1)S(1)} all-gather(bf16[64,192]{1,0:T(8,128)(2,1)S(1)} %copy-done.4), channel_id=1, replica_groups=mesh['row'=16,'col'=32] {'col'}, dimensions={0}, use_global_device_ids=true | all-gather | bytes 811008 | tf_op jit(solution)/shard_map/all_gather | solution.py:39
  592.5 57.8 %all_gather.27 = bf16[2048,192]{1,0:T(8,128)(2,1)S(1)} all-gather(bf16[64,192]{1,0:T(8,128)(2,1)S(1)} %copy-done.5), channel_id=1, replica_groups=mesh['row'=16,'col'=32] {'col'}, dimensions={0}, use_global_device_ids=true | all-gather | bytes 811008 | tf_op jit(solution)/shard_map/all_gather | solution.py:40
  650.3 4.4 convolution_bitcast_fusion.1
  654.7 2.2 convolution_bitcast_fusion
  656.8 2.4 convolution_bitcast_fusion.3
  659.2 2.4 convolution_bitcast_fusion.2
  (21 shorter events, 0.1 us)
Async XLA Ops:
  7.2 110.6 %copy-start = (bf16[192,924]{1,0:T(8,128)(2,1)S(1)}, bf16[192,924]{1,0:T(8,128)(2,1)}, u32[]{:S(2)}) copy-start(bf16[192,924]{1,0:T(8,128)(2,1)} %param.17) | copy-start | bytes 1064452
  7.2 110.5 %all-gather.4.cloned.1.call-start = ((), (), s32[]{:S(2)}) async-start(), calls=%async_computation.3 | async-start | bytes 4038656 | tf_op jit(solution)/shard_map/all_gather | solution.py:43
  9.5 222.2 %all-gather.8.cloned.1.call-start = ((), (), s32[]{:S(2)}) async-start(), calls=%async_computation.6 | async-start | bytes 4038656 | tf_op jit(solution)/shard_map/all_gather | solution.py:45
  10.3 221.5 %copy-start.6 = (bf16[192,924]{1,0:T(8,128)(2,1)S(1)}, bf16[192,924]{1,0:T(8,128)(2,1)}, u32[]{:S(2)}) copy-start(bf16[192,924]{1,0:T(8,128)(2,1)} %param.19) | copy-start | bytes 1064452
  10.3 343.6 %reduce-scatter.4.cloned.1.call-start = ((), (), s32[]{:S(2)}) async-start(), calls=%async_computation.4 | async-start | bytes 1081344 | tf_op jit(solution)/shard_map/reduce_scatter | solution.py:51
  122.3 292.7 %copy-start.2 = (bf16[256,192]{0,1:T(8,128)(2,1)S(1)}, bf16[256,192]{0,1:T(8,128)(2,1)}, u32[]{:S(2)}) copy-start(bf16[256,192]{0,1:T(8,128)(2,1)} %param.16) | copy-start | bytes 294916
  122.3 344.2 %reduce-scatter.6.cloned.1.call-start = ((), (), s32[]{:S(2)}) async-start(), calls=%async_computation.7 | async-start | bytes 1081344 | tf_op jit(solution)/shard_map/reduce_scatter | solution.py:54
  236.1 298.6 %copy-start.3 = (bf16[256,192]{0,1:T(8,128)(2,1)S(1)}, bf16[256,192]{0,1:T(8,128)(2,1)}, u32[]{:S(2)}) copy-start(bf16[256,192]{0,1:T(8,128)(2,1)} %param.18) | copy-start | bytes 294916
  236.2 420.7 %all-gather.6.cloned.1.call-start = ((), (), s32[]{:S(2)}) async-start(), calls=%async_computation.5 | async-start | bytes 1114112 | tf_op jit(solution)/shard_map/all_gather | solution.py:62
  236.8 424.8 %reduce-scatter.8.cloned.1.call-start = ((), (), s32[]{:S(2)}) async-start(), calls=%async_computation.8 | async-start | bytes 1114112 | tf_op jit(solution)/shard_map/reduce_scatter | solution.py:71
  416.8 121.0 %copy-start.4 = (bf16[64,192]{1,0:T(8,128)(2,1)S(1)}, bf16[64,192]{1,0:T(8,128)(2,1)}, u32[]{:S(2)}) copy-start(bf16[64,192]{1,0:T(8,128)(2,1)} %param.11) | copy-start | bytes 73732
  416.8 175.7 %copy-start.5 = (bf16[64,192]{1,0:T(8,128)(2,1)S(1)}, bf16[64,192]{1,0:T(8,128)(2,1)}, u32[]{:S(2)}) copy-start(bf16[64,192]{1,0:T(8,128)(2,1)} %param.12) | copy-start | bytes 73732
  650.3 4.4 copy-start.1
Sparse Core Ops, SparseCore 0:
  10.6 107.0 all-gather.3
  120.3 111.3 all-gather.7
  236.1 117.7 reduce-scatter.3
  358.7 107.7 reduce-scatter.5
  468.4 74.3 all-gather.5
  546.1 90.1 reduce-scatter.7
where the time goes:
time: 669 us; the launch traced here: 668 us
  waiting for transfers between devices  385 us (58%)
  blocking collectives  242 us (36%)
  matrix products  25 us (4%)
  between operations  14.2 us (2%)
    reduce_scatter x1, waiting for transfers between devices, on_device(): lax.psum_scatter(gate_part.astype(jnp.bfloat16), 'col', scatter_dimension...  117 us
    all_gather x1, waiting for transfers between devices, on_device(): lax.all_gather(up_grad, 'row', axis=0, tiled=True)  109 us
    all_gather x1, waiting for transfers between devices, on_device(): lax.all_gather(gate_grad, 'row', axis=0, tiled=True)  107 us
    all_gather x1, blocking collectives, on_device(): lax.all_gather(up_share.astype(jnp.bfloat16), 'col', axis=0, tiled=True)  68.2 us
    all_gather x1, blocking collectives, on_device(): lax.all_gather(gate_share.astype(jnp.bfloat16), 'col', axis=0, tiled=True)  61 us
    all_gather x1, blocking collectives, on_device(): lax.all_gather(rank_up, 'col', axis=0, tiled=True)  57.8 us
    all_gather x1, blocking collectives, on_device(): lax.all_gather(rank_gate, 'col', axis=0, tiled=True)  54.8 us
    reduce_scatter x1, waiting for transfers between devices, on_device(): lax.psum_scatter(up_part.astype(jnp.bfloat16), 'col', scatter_dimension=0...  49.7 us
  transfers between devices with their start and end apart: 6, of which 4 were waited for; matrix products, arithmetic and copies ran while one was open for 4% of the time, Pallas kernels for 0%

commit v1 on v0

v1 whole, which is shorter than its diff:
```python
import jax
import jax.numpy as jnp
from jax import lax
from jax.sharding import Mesh
from jax.sharding import PartitionSpec as P

F32 = jnp.float32
BF16 = jnp.bfloat16
RING = (0, 2, 3, 1)
SPOT = (0, 3, 1, 2)


def swiglu_back(gate_pre, up_pre, hidden_grad):
    gate_val = gate_pre.astype(F32)
    up_val = up_pre.astype(F32)
    grad_val = hidden_grad.astype(F32)
    logistic = jax.nn.sigmoid(gate_val)
    gate_grad = (grad_val * up_val * logistic * (1.0 + gate_val * (1.0 - logistic))).astype(BF16)
    up_grad = (grad_val * gate_val * logistic).astype(BF16)
    return (gate_grad, up_grad)


def turn(value, axis, step):
    return lax.ppermute(value, axis, [(i, (i + step) % 4) for i in range(4)])


def turn_z(value, step):
    return lax.ppermute(value, "zl", [(RING[i], RING[(i + step) % 4]) for i in range(4)])


def ring(value, move):
    blocks = [value]
    for _ in range(3):
        blocks.append(move(blocks[-1]))
    return blocks


def place_rank(rank, way):
    pairs = []
    for x in range(4):
        for zl in range(4):
            for zh in range(4):
                for y in range(4):
                    for c in range(2):
                        from_y = RING[(SPOT[zl] - y) % 4]
                        from_x = (x - way * zh) % 4
                        source = (((from_x * 4 + zl) * 4 + x) * 4 + from_y) * 2 + c
                        target = (((x * 4 + zl) * 4 + zh) * 4 + y) * 2 + c
                        pairs.append((source, target))
    return lax.ppermute(rank, ("x", "zl", "zh", "y", "c"), pairs)


def spread(value, axis):
    me = lax.axis_index(axis)
    stack = jnp.stack([value] + [turn(value, axis, k) for k in (1, 2, 3)])
    order = (me - jnp.arange(4)) % 4
    return stack[order]


def gather_rank(rank, way):
    piece = place_rank(rank, way)
    whole = lax.all_gather(piece, "zh")
    whole = lax.all_gather(whole, "y")
    whole = lax.all_gather(whole, "c")
    return whole.transpose(2, 1, 0, 3, 4).reshape(4, 512, 192)


def sum_over(value, axis):
    me = lax.axis_index(axis)
    total = lax.dynamic_index_in_dim(value, me, 0, keepdims=False)
    for k in (1, 2, 3):
        block = lax.dynamic_index_in_dim(value, (me + k) % 4, 0, keepdims=False)
        total = total + turn(block.astype(BF16), axis, k).astype(F32)
    return total


def reduce_col(part):
    me = lax.axis_index("c")
    halves = part.reshape(2, 256, 768)
    away = lax.dynamic_index_in_dim(halves, 1 - me, 0, keepdims=False).astype(BF16)
    mine = lax.dynamic_index_in_dim(halves, me, 0, keepdims=False)
    mine = mine + lax.ppermute(away, "c", [(0, 1), (1, 0)]).astype(F32)
    mine = sum_over(mine.reshape(4, 64, 768), "y")
    mine = sum_over(mine.reshape(4, 16, 768), "zh").astype(BF16)
    whole = lax.all_gather(mine, "zh", axis=0, tiled=True)
    whole = lax.all_gather(whole, "y", axis=0, tiled=True)
    return lax.all_gather(whole, "c", axis=0, tiled=True)


def on_device(
    layer_input,
    rank_gate,
    rank_up,
    gate_pre,
    up_pre,
    hidden_grad,
    gate_inner,
    gate_outer,
    up_inner,
    up_outer,
):
    gate_grad, up_grad = swiglu_back(gate_pre, up_pre, hidden_grad)
    ways = (1, -1)
    outers = [ring(w, lambda v, s=s: turn(v, "x", s)) for w, s in zip((gate_outer, up_outer), ways)]
    grads = [ring(g, lambda v: turn_z(v, 1)) for g in (gate_grad, up_grad)]
    ranks = [gather_rank(r, s) for r, s in zip((rank_gate, rank_up), ways)]
    inners = [ring(w, lambda v, s=s: turn(v, "x", s)) for w, s in zip((gate_inner, up_inner), ways)]
    inputs = jnp.concatenate(ring(layer_input, lambda v: turn_z(v, 1)), axis=0)

    outer_grads = []
    rank_grads = []
    for outer, grad, rank, way in zip(outers, grads, ranks, ways):
        grad = jnp.concatenate(grad, axis=0)
        outer = jnp.concatenate(outer, axis=0)
        part = jnp.einsum("tf,rf->tr", grad, outer, preferred_element_type=F32)
        rank_grads.append(reduce_col(part))
        total = jnp.einsum("tr,tf->rf", rank[0], grad, preferred_element_type=F32)
        for s in (1, 2, 3):
            other = jnp.einsum("tr,tf->rf", rank[s], grad, preferred_element_type=F32)
            total = total + turn(other.astype(BF16), "x", -s * way).astype(F32)
        outer_grads.append(total)

    inner_grads = []
    back = 0.0
    for inner, rank_grad, way in zip(inners, rank_grads, ways):
        inner = jnp.concatenate(inner, axis=1)
        back = back + jnp.einsum("tr,dr->td", rank_grad, inner, preferred_element_type=F32)
        part = jnp.einsum("td,tr->dr", inputs, rank_grad, preferred_element_type=F32)
        total = part[:, :192]
        for s in (1, 2, 3):
            other = part[:, 192 * s : 192 * (s + 1)].astype(BF16)
            total = total + turn(other, "x", -s * way).astype(F32)
        inner_grads.append(total)
    input_grad = back[:128]
    for s in (1, 2, 3):
        other = back[128 * s : 128 * (s + 1)].astype(BF16)
        input_grad = input_grad + turn_z(other, -s).astype(F32)
    return (
        inner_grads[0],
        outer_grads[0],
        inner_grads[1],
        outer_grads[1],
        input_grad.astype(BF16),
    )


def solution(mesh):
    grid = Mesh(mesh.devices.reshape(4, 4, 4, 4, 2), ("x", "zl", "zh", "y", "c"))
    row = ("x", "zl")
    col = ("zh", "y", "c")
    return jax.shard_map(
        on_device,
        mesh=grid,
        in_specs=(
            P(row, col),
            P(col, row),
            P(col, row),
            P(row, col),
            P(row, col),
            P(row, col),
            P(col, row),
            P(row, col),
            P(col, row),
            P(row, col),
        ),
        out_specs=(
            P(col, row),
            P(row, col),
            P(col, row),
            P(row, col),
            P(row, col),
        ),
        check_vma=False,
    )
```

time: 669 us -> 387 us (0.58)
  the two profiles are of different devices: /device:TPU:65 before, /device:TPU:32 now
where the time goes in v1:
time: 387 us; the launch traced here: 385 us
  starting transfers between devices  189 us (49%)
  blocking collectives  146 us (38%)
  waiting for transfers between devices  33.8 us (9%)
  matrix products  9.27 us (2%)
    ppermute x36, starting transfers between devices, turn(): return lax.ppermute(value, axis, [(i, (i + step) % 4) for i in range(4)])  134 us
    all_gather x2, blocking collectives, gather_rank(): whole = lax.all_gather(piece, 'zh')  49.4 us
    ppermute x12, starting transfers between devices, turn_z(): lax.ppermute(value, 'zl', [(RING[i], RING[(i + step) % 4]) for i in range...  40.8 us
    all_gather x2, blocking collectives, reduce_col(): whole = lax.all_gather(mine, 'zh', axis=0, tiled=True)  34.9 us
    all_gather x2, blocking collectives, gather_rank(): whole = lax.all_gather(whole, 'y')  26.3 us
    all_gather x2, blocking collectives, reduce_col(): whole = lax.all_gather(whole, 'y', axis=0, tiled=True)  25 us
    ppermute x36, waiting for transfers between devices, turn(): return lax.ppermute(value, axis, [(i, (i + step) % 4) for i in range(4)])  20.6 us
    ppermute x12, waiting for transfers between devices, turn_z(): lax.ppermute(value, 'zl', [(RING[i], RING[(i + step) % 4]) for i in range...  12.2 us
  transfers between devices with their start and end apart: 52, of which 8 were waited for; matrix products, arithmetic and copies ran while one was open for 3% of the time, Pallas kernels for 0%

profile of v1, /device:TPU:32, one launch (start us, length us, event | category | flops | bytes accessed | tf_op | source)
XLA Modules:
  0.0 385.4 jit_solution(5560603279786636706)
XLA Ops:
  2.1 7.5 %collective-permute-start.3 = (bf16[128,924]{0,1:T(8,128)(2,1)S(1)}, bf16[128,924]{0,1:T(8,128)(2,1)S(1)}, u32[]{:S(2)}, u32[]{:S(2)}) collective-permute-start(bf16[128,924]{0,1:T(8,128)(2,1)S(1)} %get-tuple-element.40), channel_id=1, source_target_pairs={{0,64},{64,96},{96,32},{32,0},{1,65},{65,97},{97,33},{33,1},{2,66}... | collective-permute-start | bytes 709640 | tf_op jit(solution)/shard_map/ppermute | solution.py:28
  16.7 4.9 %collective-permute-start.39 = (bf16[64,192]{1,0:T(8,128)(2,1)}, bf16[64,192]{1,0:T(8,128)(2,1)S(1)}, u32[]{:S(2)}, u32[]{:S(2)}) collective-permute-start(bf16[64,192]{1,0:T(8,128)(2,1)} %param.12), channel_id=1, source_target_pairs={{0,0},{1,1},{2,2},{3,3},{6,4},{7,5},{4,6},{5,7},{128,8},{129,9},{1... | collective-permute-start | bytes 73736 | tf_op jit(solution)/shard_map/ppermute | solution.py:50
  23.5 5.3 %collective-permute-start.19 = (bf16[64,192]{1,0:T(8,128)(2,1)}, bf16[64,192]{1,0:T(8,128)(2,1)S(1)}, u32[]{:S(2)}, u32[]{:S(2)}) collective-permute-start(bf16[64,192]{1,0:T(8,128)(2,1)} %param.11), channel_id=1, source_target_pairs={{0,0},{1,1},{2,2},{3,3},{6,4},{7,5},{4,6},{5,7},{384,8},{385,9},{3... | collective-permute-start | bytes 73736 | tf_op jit(solution)/shard_map/ppermute | solution.py:50
  28.8 31.6 %all-gather.3 = bf16[256,192]{1,0:T(8,128)(2,1)S(1)} all-gather(bf16[64,192]{1,0:T(8,128)(2,1)S(1)} %collective-permute-done.39), channel_id=5, replica_groups=mesh['x'=4,'zl'=4,'zh'=4,'y'=4,'c'=2] {'zh'}, dimensions={0}, use_global_device_ids=true | all-gather | bytes 122880 | tf_op jit(solution)/shard_map/all_gather | solution.py:62
  60.4 13.6 %all-gather.4 = bf16[16,64,192]{2,1,0:T(8,128)(2,1)S(1)} all-gather(bf16[4,64,192]{2,1,0:T(8,128)(2,1)S(1)} %bitcast.138), channel_id=6, replica_groups=mesh['x'=4,'zl'=4,'zh'=4,'y'=4,'c'=2] {'y'}, dimensions={0}, use_global_device_ids=true | all-gather | bytes 491520 | tf_op jit(solution)/shard_map/all_gather | solution.py:63
  80.4 17.8 %all-gather = bf16[256,192]{1,0:T(8,128)(2,1)S(1)} all-gather(bf16[64,192]{1,0:T(8,128)(2,1)S(1)} %collective-permute-done.19), channel_id=2, replica_groups=mesh['x'=4,'zl'=4,'zh'=4,'y'=4,'c'=2] {'zh'}, dimensions={0}, use_global_device_ids=true | all-gather | bytes 122880 | tf_op jit(solution)/shard_map/all_gather | solution.py:62
  98.2 12.8 %all-gather.1 = bf16[16,64,192]{2,1,0:T(8,128)(2,1)S(1)} all-gather(bf16[4,64,192]{2,1,0:T(8,128)(2,1)S(1)} %bitcast.139), channel_id=3, replica_groups=mesh['x'=4,'zl'=4,'zh'=4,'y'=4,'c'=2] {'y'}, dimensions={0}, use_global_device_ids=true | all-gather | bytes 491520 | tf_op jit(solution)/shard_map/all_gather | solution.py:63
  119.7 5.3 %collective-permute-start.4 = (bf16[128,924]{0,1:T(8,128)(2,1)S(1)}, bf16[128,924]{0,1:T(8,128)(2,1)S(1)}, u32[]{:S(2)}, u32[]{:S(2)}) collective-permute-start(bf16[128,924]{0,1:T(8,128)(2,1)S(1)} %collective-permute-done.3), channel_id=1, source_target_pairs={{0,64},{64,96},{96,32},{32,0},{1,65},{65,97},{97,33},{33,1},{2,66}... | collective-permute-start | bytes 709640 | tf_op jit(solution)/shard_map/ppermute | solution.py:28
  130.8 7.1 %collective-permute-done.2 = bf16[128,256]{1,0:T(8,128)(2,1)S(1)} collective-permute-done((bf16[128,256]{1,0:T(8,128)(2,1)S(1)}, bf16[128,256]{1,0:T(8,128)(2,1)S(1)}, u32[]{:S(2)}, u32[]{:S(2)}) %collective-permute-start.2) | collective-permute-done | bytes 65568 | tf_op jit(solution)/shard_map/ppermute | solution.py:28
  137.8 10.7 %collective-permute-start.46 = (bf16[256,192]{0,1:T(8,128)(2,1)S(1)}, bf16[256,192]{0,1:T(8,128)(2,1)S(1)}, u32[]{:S(2)}, u32[]{:S(2)}) collective-permute-start(bf16[256,192]{0,1:T(8,128)(2,1)S(1)} %copy-done.2), channel_id=1, source_target_pairs={{0,384},{128,0},{256,128},{384,256},{1,385},{129,1},{257,129},{385... | collective-permute-start | bytes 294920 | tf_op jit(solution)/shard_map/ppermute | solution.py:24
  152.5 5.1 %collective-permute-start.27 = (bf16[192,924]{1,0:T(8,128)(2,1)S(1)}, bf16[192,924]{1,0:T(8,128)(2,1)S(1)}, u32[]{:S(2)}, u32[]{:S(2)}) collective-permute-start(bf16[192,924]{1,0:T(8,128)(2,1)S(1)} %collective-permute-done.26), channel_id=1, source_target_pairs={{0,384},{128,0},{256,128},{384,256},{1,385},{129,1},{257,129},{385... | collective-permute-start | bytes 1064456 | tf_op jit(solution)/shard_map/ppermute | solution.py:24
  177.1 9.8 %collective-permute-done.8 = bf16[192,924]{1,0:T(8,128)(2,1)S(1)} collective-permute-done((bf16[192,924]{1,0:T(8,128)(2,1)S(1)}, bf16[192,924]{1,0:T(8,128)(2,1)S(1)}, u32[]{:S(2)}, u32[]{:S(2)}) %collective-permute-start.8) | collective-permute-done | bytes 354848 | tf_op jit(solution)/shard_map/ppermute | solution.py:24
  202.9 5.1 %collective-permute-start.20 = (bf16[192,924]{1,0:T(8,128)(2,1)S(1)}, bf16[192,924]{1,0:T(8,128)(2,1)S(1)}, u32[]{:S(2)}, u32[]{:S(2)}) collective-permute-start(bf16[192,924]{1,0:T(8,128)(2,1)S(1)} %fusion.22), channel_id=1, source_target_pairs={{0,384},{128,0},{256,128},{384,256},{1,385},{129,1},{257,129},{385... | collective-permute-start | bytes 1064456 | tf_op jit(solution)/shard_map/ppermute | solution.py:24
  251.9 7.3 %collective-permute-start.34 = (bf16[16,768]{1,0:T(8,128)(2,1)S(1)}, bf16[16,768]{1,0:T(8,128)(2,1)S(1)}, u32[]{:S(2)}, u32[]{:S(2)}) collective-permute-start(bf16[16,768]{1,0:T(8,128)(2,1)S(1)} %get-tuple-element.52), channel_id=1, source_target_pairs={{0,16},{8,24},{16,0},{24,8},{1,17},{9,25},{17,1},{25,9},{2,18},{10... | collective-permute-start | bytes 73736 | tf_op jit(solution)/shard_map/ppermute | solution.py:24
  259.2 6.8 %collective-permute-start.35 = (bf16[16,768]{1,0:T(8,128)(2,1)S(1)}, bf16[16,768]{1,0:T(8,128)(2,1)S(1)}, u32[]{:S(2)}, u32[]{:S(2)}) collective-permute-start(bf16[16,768]{1,0:T(8,128)(2,1)S(1)} %get-tuple-element.51), channel_id=1, source_target_pairs={{0,24},{8,0},{16,8},{24,16},{1,25},{9,1},{17,9},{25,17},{2,26},{10... | collective-permute-start | bytes 73736 | tf_op jit(solution)/shard_map/ppermute | solution.py:24
  269.0 7.3 %collective-permute-start.14 = (bf16[16,768]{1,0:T(8,128)(2,1)S(1)}, bf16[16,768]{1,0:T(8,128)(2,1)S(1)}, u32[]{:S(2)}, u32[]{:S(2)}) collective-permute-start(bf16[16,768]{1,0:T(8,128)(2,1)S(1)} %get-tuple-element.55), channel_id=1, source_target_pairs={{0,16},{8,24},{16,0},{24,8},{1,17},{9,25},{17,1},{25,9},{2,18},{10... | collective-permute-start | bytes 73736 | tf_op jit(solution)/shard_map/ppermute | solution.py:24
  276.3 6.8 %collective-permute-start.15 = (bf16[16,768]{1,0:T(8,128)(2,1)S(1)}, bf16[16,768]{1,0:T(8,128)(2,1)S(1)}, u32[]{:S(2)}, u32[]{:S(2)}) collective-permute-start(bf16[16,768]{1,0:T(8,128)(2,1)S(1)} %get-tuple-element.54), channel_id=1, source_target_pairs={{0,24},{8,0},{16,8},{24,16},{1,25},{9,1},{17,9},{25,17},{2,26},{10... | collective-permute-start | bytes 73736 | tf_op jit(solution)/shard_map/ppermute | solution.py:24
  283.1 17.5 %all_gather.63 = bf16[64,768]{1,0:T(8,128)(2,1)S(1)} all-gather(bf16[16,768]{1,0:T(8,128)(2,1)S(1)} %fusion.73), channel_id=1, replica_groups=mesh['x'=4,'zl'=4,'zh'=4,'y'=4,'c'=2] {'zh'}, dimensions={0}, use_global_device_ids=true | all-gather | bytes 122880 | tf_op jit(solution)/shard_map/all_gather | solution.py:85
  300.6 12.5 %all_gather.64 = bf16[256,768]{1,0:T(8,128)(2,1)S(1)} all-gather(bf16[64,768]{1,0:T(8,128)(2,1)S(1)} %all_gather.63), channel_id=1, replica_groups=mesh['x'=4,'zl'=4,'zh'=4,'y'=4,'c'=2] {'y'}, dimensions={0}, use_global_device_ids=true | all-gather | bytes 491520 | tf_op jit(solution)/shard_map/all_gather | solution.py:86
  315.5 17.4 %all_gather.54 = bf16[64,768]{1,0:T(8,128)(2,1)S(1)} all-gather(bf16[16,768]{1,0:T(8,128)(2,1)S(1)} %fusion.76), channel_id=1, replica_groups=mesh['x'=4,'zl'=4,'zh'=4,'y'=4,'c'=2] {'zh'}, dimensions={0}, use_global_device_ids=true | all-gather | bytes 122880 | tf_op jit(solution)/shard_map/all_gather | solution.py:85
  332.9 12.5 %all_gather.55 = bf16[256,768]{1,0:T(8,128)(2,1)S(1)} all-gather(bf16[64,768]{1,0:T(8,128)(2,1)S(1)} %all_gather.54), channel_id=1, replica_groups=mesh['x'=4,'zl'=4,'zh'=4,'y'=4,'c'=2] {'y'}, dimensions={0}, use_global_device_ids=true | all-gather | bytes 491520 | tf_op jit(solution)/shard_map/all_gather | solution.py:86
  360.6 5.2 %collective-permute-start.37 = (bf16[256,192]{1,0:T(8,128)(2,1)S(1)}, bf16[256,192]{1,0:T(8,128)(2,1)S(1)}, u32[]{:S(2)}, u32[]{:S(2)}) collective-permute-start(bf16[256,192]{1,0:T(8,128)(2,1)S(1)} %get-tuple-element.43), channel_id=1, source_target_pairs={{0,256},{128,384},{256,0},{384,128},{1,257},{129,385},{257,1},{385... | collective-permute-start | bytes 294920 | tf_op jit(solution)/shard_map/ppermute | solution.py:24
  370.6 5.2 %collective-permute-start.17 = (bf16[256,192]{1,0:T(8,128)(2,1)S(1)}, bf16[256,192]{1,0:T(8,128)(2,1)S(1)}, u32[]{:S(2)}, u32[]{:S(2)}) collective-permute-start(bf16[256,192]{1,0:T(8,128)(2,1)S(1)} %get-tuple-element.46), channel_id=1, source_target_pairs={{0,256},{128,384},{256,0},{384,128},{1,257},{129,385},{257,1},{385... | collective-permute-start | bytes 294920 | tf_op jit(solution)/shard_map/ppermute | solution.py:24
  379.5 5.1 %collective-permute-done.18 = bf16[256,192]{1,0:T(8,128)(2,1)S(1)} collective-permute-done((bf16[256,192]{1,0:T(8,128)(2,1)S(1)}, bf16[256,192]{1,0:T(8,128)(2,1)S(1)}, u32[]{:S(2)}, u32[]{:S(2)}) %collective-permute-start.18) | collective-permute-done | bytes 98336 | tf_op jit(solution)/shard_map/ppermute | solution.py:24
  (148 shorter events, 143.6 us)
Async XLA Ops:
  2.1 117.6 %collective-permute-start.3 = (bf16[128,924]{0,1:T(8,128)(2,1)S(1)}, bf16[128,924]{0,1:T(8,128)(2,1)S(1)}, u32[]{:S(2)}, u32[]{:S(2)}) collective-permute-start(bf16[128,924]{0,1:T(8,128)(2,1)S(1)} %get-tuple-element.40), channel_id=1, source_target_pairs={{0,64},{64,96},{96,32},{32,0},{1,65},{65,97},{97,33},{33,1},{2,66}... | collective-permute-start | bytes 709640 | tf_op jit(solution)/shard_map/ppermute | solution.py:28
  9.6 139.0 %collective-permute-start.6 = (bf16[192,924]{1,0:T(8,128)(2,1)}, bf16[192,924]{1,0:T(8,128)(2,1)S(1)}, u32[]{:S(2)}, u32[]{:S(2)}) collective-permute-start(bf16[192,924]{1,0:T(8,128)(2,1)} %param.17), channel_id=1, source_target_pairs={{0,128},{128,256},{256,384},{384,0},{1,129},{129,257},{257,385},{3... | collective-permute-start | bytes 1064456 | tf_op jit(solution)/shard_map/ppermute | solution.py:24
  11.5 102.0 %collective-permute-start.23 = (bf16[128,924]{0,1:T(8,128)(2,1)S(1)}, bf16[128,924]{0,1:T(8,128)(2,1)S(1)}, u32[]{:S(2)}, u32[]{:S(2)}) collective-permute-start(bf16[128,924]{0,1:T(8,128)(2,1)S(1)} %get-tuple-element.39), channel_id=1, source_target_pairs={{0,64},{64,96},{96,32},{32,0},{1,65},{65,97},{97,33},{33,1},{2,66}... | collective-permute-start | bytes 709640 | tf_op jit(solution)/shard_map/ppermute | solution.py:28
  13.5 102.4 %collective-permute-start = (bf16[128,256]{1,0:T(8,128)(2,1)}, bf16[128,256]{1,0:T(8,128)(2,1)S(1)}, u32[]{:S(2)}, u32[]{:S(2)}) collective-permute-start(bf16[128,256]{1,0:T(8,128)(2,1)} %param.10), channel_id=1, source_target_pairs={{0,64},{64,96},{96,32},{32,0},{1,65},{65,97},{97,33},{33,1},{2,66}... | collective-permute-start | bytes 196616 | tf_op jit(solution)/shard_map/ppermute | solution.py:28
  23.5 53.0 %collective-permute-start.19 = (bf16[64,192]{1,0:T(8,128)(2,1)}, bf16[64,192]{1,0:T(8,128)(2,1)S(1)}, u32[]{:S(2)}, u32[]{:S(2)}) collective-permute-start(bf16[64,192]{1,0:T(8,128)(2,1)} %param.11), channel_id=1, source_target_pairs={{0,0},{1,1},{2,2},{3,3},{6,4},{7,5},{4,6},{5,7},{384,8},{385,9},{3... | collective-permute-start | bytes 73736 | tf_op jit(solution)/shard_map/ppermute | solution.py:50
  76.5 74.0 %collective-permute-start.26 = (bf16[192,924]{1,0:T(8,128)(2,1)S(1)}, bf16[192,924]{1,0:T(8,128)(2,1)S(1)}, u32[]{:S(2)}, u32[]{:S(2)}) collective-permute-start(bf16[192,924]{1,0:T(8,128)(2,1)S(1)} %copy-done.1), channel_id=1, source_target_pairs={{0,384},{128,0},{256,128},{384,256},{1,385},{129,1},{257,129},{385... | collective-permute-start | bytes 1064456 | tf_op jit(solution)/shard_map/ppermute | solution.py:24
  119.7 32.8 %collective-permute-start.4 = (bf16[128,924]{0,1:T(8,128)(2,1)S(1)}, bf16[128,924]{0,1:T(8,128)(2,1)S(1)}, u32[]{:S(2)}, u32[]{:S(2)}) collective-permute-start(bf16[128,924]{0,1:T(8,128)(2,1)S(1)} %collective-permute-done.3), channel_id=1, source_target_pairs={{0,64},{64,96},{96,32},{32,0},{1,65},{65,97},{97,33},{33,1},{2,66}... | collective-permute-start | bytes 709640 | tf_op jit(solution)/shard_map/ppermute | solution.py:28
  125.3 32.3 %collective-permute-start.25 = (bf16[128,924]{0,1:T(8,128)(2,1)S(1)}, bf16[128,924]{0,1:T(8,128)(2,1)S(1)}, u32[]{:S(2)}, u32[]{:S(2)}) collective-permute-start(bf16[128,924]{0,1:T(8,128)(2,1)S(1)} %collective-permute-done.24), channel_id=1, source_target_pairs={{0,64},{64,96},{96,32},{32,0},{1,65},{65,97},{97,33},{33,1},{2,66}... | collective-permute-start | bytes 709640 | tf_op jit(solution)/shard_map/ppermute | solution.py:28
  137.8 56.8 %collective-permute-start.46 = (bf16[256,192]{0,1:T(8,128)(2,1)S(1)}, bf16[256,192]{0,1:T(8,128)(2,1)S(1)}, u32[]{:S(2)}, u32[]{:S(2)}) collective-permute-start(bf16[256,192]{0,1:T(8,128)(2,1)S(1)} %copy-done.2), channel_id=1, source_target_pairs={{0,384},{128,0},{256,128},{384,256},{1,385},{129,1},{257,129},{385... | collective-permute-start | bytes 294920 | tf_op jit(solution)/shard_map/ppermute | solution.py:24
  148.6 48.1 %collective-permute-start.43 = (bf16[256,192]{0,1:T(8,128)(2,1)S(1)}, bf16[256,192]{0,1:T(8,128)(2,1)S(1)}, u32[]{:S(2)}, u32[]{:S(2)}) collective-permute-start(bf16[256,192]{0,1:T(8,128)(2,1)S(1)} %copy-done.3), channel_id=1, source_target_pairs={{0,128},{128,256},{256,384},{384,0},{1,129},{129,257},{257,385},{3... | collective-permute-start | bytes 294920 | tf_op jit(solution)/shard_map/ppermute | solution.py:24
  152.5 19.5 %collective-permute-start.27 = (bf16[192,924]{1,0:T(8,128)(2,1)S(1)}, bf16[192,924]{1,0:T(8,128)(2,1)S(1)}, u32[]{:S(2)}, u32[]{:S(2)}) collective-permute-start(bf16[192,924]{1,0:T(8,128)(2,1)S(1)} %collective-permute-done.26), channel_id=1, source_target_pairs={{0,384},{128,0},{256,128},{384,256},{1,385},{129,1},{257,129},{385... | collective-permute-start | bytes 1064456 | tf_op jit(solution)/shard_map/ppermute | solution.py:24
  166.7 34.3 %collective-permute-start.40 = (bf16[192,924]{1,0:T(8,128)(2,1)S(1)}, bf16[192,924]{1,0:T(8,128)(2,1)S(1)}, u32[]{:S(2)}, u32[]{:S(2)}) collective-permute-start(bf16[192,924]{1,0:T(8,128)(2,1)S(1)} %fusion.25), channel_id=1, source_target_pairs={{0,128},{128,256},{256,384},{384,0},{1,129},{129,257},{257,385},{3... | collective-permute-start | bytes 1064456 | tf_op jit(solution)/shard_map/ppermute | solution.py:24
  196.7 19.6 %collective-permute-start.47 = (bf16[256,192]{0,1:T(8,128)(2,1)S(1)}, bf16[256,192]{0,1:T(8,128)(2,1)S(1)}, u32[]{:S(2)}, u32[]{:S(2)}) collective-permute-start(bf16[256,192]{0,1:T(8,128)(2,1)S(1)} %collective-permute-done.46), channel_id=1, source_target_pairs={{0,384},{128,0},{256,128},{384,256},{1,385},{129,1},{257,129},{385... | collective-permute-start | bytes 294920 | tf_op jit(solution)/shard_map/ppermute | solution.py:24
  202.9 22.0 %collective-permute-start.20 = (bf16[192,924]{1,0:T(8,128)(2,1)S(1)}, bf16[192,924]{1,0:T(8,128)(2,1)S(1)}, u32[]{:S(2)}, u32[]{:S(2)}) collective-permute-start(bf16[192,924]{1,0:T(8,128)(2,1)S(1)} %fusion.22), channel_id=1, source_target_pairs={{0,384},{128,0},{256,128},{384,256},{1,385},{129,1},{257,129},{385... | collective-permute-start | bytes 1064456 | tf_op jit(solution)/shard_map/ppermute | solution.py:24
  213.4 21.3 %collective-permute-start.22 = (bf16[192,924]{1,0:T(8,128)(2,1)S(1)}, bf16[192,924]{1,0:T(8,128)(2,1)S(1)}, u32[]{:S(2)}, u32[]{:S(2)}) collective-permute-start(bf16[192,924]{1,0:T(8,128)(2,1)S(1)} %fusion.24), channel_id=1, source_target_pairs={{0,128},{128,256},{256,384},{384,0},{1,129},{129,257},{257,385},{3... | collective-permute-start | bytes 1064456 | tf_op jit(solution)/shard_map/ppermute | solution.py:24
  216.3 21.8 %collective-permute-start.10 = (bf16[64,768]{1,0:T(8,128)(2,1)S(1)}, bf16[64,768]{1,0:T(8,128)(2,1)S(1)}, u32[]{:S(2)}, u32[]{:S(2)}) collective-permute-start(bf16[64,768]{1,0:T(8,128)(2,1)S(1)} %get-tuple-element.36), channel_id=1, source_target_pairs={{0,2},{2,4},{4,6},{6,0},{1,3},{3,5},{5,7},{7,1},{8,10},{10,12},{12... | collective-permute-start | bytes 294920 | tf_op jit(solution)/shard_map/ppermute | solution.py:24
  218.6 24.3 %collective-permute-start.11 = (bf16[64,768]{1,0:T(8,128)(2,1)S(1)}, bf16[64,768]{1,0:T(8,128)(2,1)S(1)}, u32[]{:S(2)}, u32[]{:S(2)}) collective-permute-start(bf16[64,768]{1,0:T(8,128)(2,1)S(1)} %get-tuple-element.38), channel_id=1, source_target_pairs={{0,4},{2,6},{4,0},{6,2},{1,5},{3,7},{5,1},{7,3},{8,12},{10,14},{12... | collective-permute-start | bytes 294920 | tf_op jit(solution)/shard_map/ppermute | solution.py:24
  224.9 20.5 %collective-permute-start.12 = (bf16[64,768]{1,0:T(8,128)(2,1)S(1)}, bf16[64,768]{1,0:T(8,128)(2,1)S(1)}, u32[]{:S(2)}, u32[]{:S(2)}) collective-permute-start(bf16[64,768]{1,0:T(8,128)(2,1)S(1)} %get-tuple-element.37), channel_id=1, source_target_pairs={{0,6},{2,0},{4,2},{6,4},{1,7},{3,1},{5,3},{7,5},{8,14},{10,8},{12,... | collective-permute-start | bytes 294920 | tf_op jit(solution)/shard_map/ppermute | solution.py:24
  228.3 20.4 %collective-permute-start.30 = (bf16[64,768]{1,0:T(8,128)(2,1)S(1)}, bf16[64,768]{1,0:T(8,128)(2,1)S(1)}, u32[]{:S(2)}, u32[]{:S(2)}) collective-permute-start(bf16[64,768]{1,0:T(8,128)(2,1)S(1)} %get-tuple-element.33), channel_id=1, source_target_pairs={{0,2},{2,4},{4,6},{6,0},{1,3},{3,5},{5,7},{7,1},{8,10},{10,12},{12... | collective-permute-start | bytes 294920 | tf_op jit(solution)/shard_map/ppermute | solution.py:24
  242.9 105.8 %collective-permute-start.48 = (bf16[256,192]{0,1:T(8,128)(2,1)S(1)}, bf16[256,192]{0,1:T(8,128)(2,1)S(1)}, u32[]{:S(2)}, u32[]{:S(2)}) collective-permute-start(bf16[256,192]{0,1:T(8,128)(2,1)S(1)} %collective-permute-done.47), channel_id=1, source_target_pairs={{0,384},{128,0},{256,128},{384,256},{1,385},{129,1},{257,129},{385... | collective-permute-start | bytes 294920 | tf_op jit(solution)/shard_map/ppermute | solution.py:24
  245.4 103.7 %collective-permute-start.45 = (bf16[256,192]{0,1:T(8,128)(2,1)S(1)}, bf16[256,192]{0,1:T(8,128)(2,1)S(1)}, u32[]{:S(2)}, u32[]{:S(2)}) collective-permute-start(bf16[256,192]{0,1:T(8,128)(2,1)S(1)} %collective-permute-done.44), channel_id=1, source_target_pairs={{0,128},{128,256},{256,384},{384,0},{1,129},{129,257},{257,385},{3... | collective-permute-start | bytes 294920 | tf_op jit(solution)/shard_map/ppermute | solution.py:24
  266.0 49.5 %collective-permute-start.13 = (bf16[16,768]{1,0:T(8,128)(2,1)S(1)}, bf16[16,768]{1,0:T(8,128)(2,1)S(1)}, u32[]{:S(2)}, u32[]{:S(2)}) collective-permute-start(bf16[16,768]{1,0:T(8,128)(2,1)S(1)} %get-tuple-element.53), channel_id=1, source_target_pairs={{0,8},{8,16},{16,24},{24,0},{1,9},{9,17},{17,25},{25,1},{2,10},{10... | collective-permute-start | bytes 73736 | tf_op jit(solution)/shard_map/ppermute | solution.py:24
  269.0 46.5 %collective-permute-start.14 = (bf16[16,768]{1,0:T(8,128)(2,1)S(1)}, bf16[16,768]{1,0:T(8,128)(2,1)S(1)}, u32[]{:S(2)}, u32[]{:S(2)}) collective-permute-start(bf16[16,768]{1,0:T(8,128)(2,1)S(1)} %get-tuple-element.55), channel_id=1, source_target_pairs={{0,16},{8,24},{16,0},{24,8},{1,17},{9,25},{17,1},{25,9},{2,18},{10... | collective-permute-start | bytes 73736 | tf_op jit(solution)/shard_map/ppermute | solution.py:24
  276.3 39.2 %collective-permute-start.15 = (bf16[16,768]{1,0:T(8,128)(2,1)S(1)}, bf16[16,768]{1,0:T(8,128)(2,1)S(1)}, u32[]{:S(2)}, u32[]{:S(2)}) collective-permute-start(bf16[16,768]{1,0:T(8,128)(2,1)S(1)} %get-tuple-element.54), channel_id=1, source_target_pairs={{0,24},{8,0},{16,8},{24,16},{1,25},{9,1},{17,9},{25,17},{2,26},{10... | collective-permute-start | bytes 73736 | tf_op jit(solution)/shard_map/ppermute | solution.py:24
  (32 other events, 538.3 us)

commit v2 on v1

v2 whole, which is shorter than its diff:
```python
import jax
import jax.numpy as jnp
from jax import lax
from jax.experimental import pallas as pl
from jax.experimental.pallas import tpu as pltpu
from jax.sharding import Mesh
from jax.sharding import PartitionSpec as P

F32 = jnp.float32
BF16 = jnp.bfloat16
RING = (0, 2, 3, 1)
FF = 924
PAD = 928
WIDE = 1024


def swiglu_back(gate_pre, up_pre, hidden_grad):
    gate_val = gate_pre.astype(F32)
    up_val = up_pre.astype(F32)
    grad_val = hidden_grad.astype(F32)
    logistic = jax.nn.sigmoid(gate_val)
    gate_grad = (grad_val * up_val * logistic * (1.0 + gate_val * (1.0 - logistic))).astype(BF16)
    up_grad = (grad_val * gate_val * logistic).astype(BF16)
    return (gate_grad, up_grad)


def turn(value, axis, step):
    return lax.ppermute(value, axis, [(i, (i + step) % 4) for i in range(4)])


def turn_z(value, step):
    return lax.ppermute(value, "zl", [(RING[i], RING[(i + step) % 4]) for i in range(4)])


def exchange(value, axis):
    return lax.all_to_all(value, axis, 0, 0)


def kernel_call(body, out, vmem, rest=(), limit=48):
    def run(*refs):
        body(refs[: len(vmem)], refs[len(vmem) + len(rest) :])

    return pl.pallas_call(
        run,
        out_shape=[jax.ShapeDtypeStruct(shape, dtype) for shape, dtype in out],
        in_specs=[pl.BlockSpec(memory_space=pltpu.VMEM)] * len(vmem)
        + [pl.BlockSpec(memory_space=pl.ANY)] * len(rest),
        out_specs=[pl.BlockSpec(memory_space=pltpu.VMEM)] * len(out),
        compiler_params=pltpu.CompilerParams(vmem_limit_bytes=limit * 2**20),
        cost_estimate=pl.CostEstimate(flops=1000, bytes_accessed=1000, transcendentals=0),
    )(*vmem, *rest)


def dot(left, right, dims):
    return lax.dot_general(left, right, (dims, ((), ())), preferred_element_type=F32)


def z_owner(k):
    line = lax.axis_index("zl")
    spot = jnp.where(line == 0, 0, jnp.where(line == 1, 3, line - 1))
    place = (spot - k + 4) % 4
    return jnp.where(place == 0, 0, jnp.where(place == 3, 1, place + 1))


def factor_rows(refs, s, b, columns):
    if s == 2:
        return refs[2 + b][:, columns]
    return refs[{0: 0, 1: 1, 3: 4}[s]][192 * b : 192 * (b + 1), columns]


def join(met, rest):
    def body(ins, outs):
        for k in range(4):
            columns = slice(128 * k, 128 * (k + 1))
            outs[0][:, columns] = ins[k][: 2 * PAD, :]
            outs[1][:, columns] = ins[k][2 * PAD :, :]

    return kernel_call(body, [((2 * PAD, 512), BF16), ((256, 512), BF16)], met, rest)


def hidden_sums(grads, factors):
    def body(ins, outs):
        core = lax.axis_index("c")
        for b in range(2):
            grad = ins[0][0:WIDE, :] if b == 0 else ins[0][2 * PAD - WIDE :, :]
            for s in range(4):
                part = dot(factor_rows(ins[1:], s, b, slice(0, WIDE)), grad, ((1,), (0,))).astype(BF16)

                @pl.when(core == b)
                def _():
                    outs[1][192 * s : 192 * (s + 1), :] = part

                @pl.when(core != b)
                def _():
                    outs[0][192 * s : 192 * (s + 1), :] = part

                inner = factor_rows(ins[1:], s, b, slice(WIDE, WIDE + 256))
                outs[2][s, 192 * b : 192 * (b + 1), :] = inner

    out = [((768, 512), BF16)] * 2 + [((4, 384, 256), BF16)]
    return kernel_call(body, out, [grads, *factors])


def add(left, right, rest):
    def body(ins, outs):
        outs[0][...] = (ins[0][...].astype(F32) + ins[1][...].astype(F32)).astype(BF16)

    return kernel_call(body, [(left.shape, BF16)], [left, right], rest)[0]


def sum_blocks(value, copies, rest):
    shape = value.shape[1:]

    def body(ins, outs):
        total = (ins[0][0].astype(F32) + ins[0][1].astype(F32)) + (ins[0][2].astype(F32) + ins[0][3].astype(F32))
        if copies:
            for k in range(copies):
                outs[0][k] = total.astype(BF16)
        else:
            outs[0][...] = total.astype(BF16)

    return kernel_call(body, [((copies, *shape) if copies else shape, BF16)], [value], rest)[0]


def outer_sums(grads, rank, other):
    def body(ins, outs):
        first = lax.axis_index("c") == 0
        totals = [0.0, 0.0]
        for s in range(4):
            pieces = []
            for k in range(4):
                spot = (z_owner(k), s)
                mine, away = ins[1][spot], ins[2][spot]
                pieces.append(jnp.where(first, mine, away))
                pieces.append(jnp.where(first, away, mine))
            rank_rows = jnp.concatenate(pieces, axis=0)
            for b in range(2):
                left = rank_rows[:, 192 * b : 192 * (b + 1)]
                part = dot(left, ins[0][s, PAD * b : PAD * (b + 1), :], ((0,), (1,)))
                totals[b] = totals[b] + part
        for b in range(2):
            outs[b][...] = totals[b][:, :FF]

    return kernel_call(body, [((192, FF), F32)] * 2, [grads, rank, other])


def inner_sums(inputs, mine, away, rest):
    def body(ins, outs):
        core = lax.axis_index("c")
        me = lax.axis_index("x")
        for ref, branch in ((ins[1], core), (ins[2], 1 - core)):
            rows = pl.ds(pl.multiple_of(branch * 192, 16), 192)
            for s in range(4):
                part = dot(ref[192 * s : 192 * (s + 1), :], ins[0][...], ((1,), (1,)))
                outs[0][(me - s + 4) % 4, rows, :] = part.astype(BF16)

    return kernel_call(body, [((4, 384, 256), BF16)], [inputs, mine, away], rest)[0]


def input_sums(inner, mine, away, rest):
    def body(ins, outs):
        core = lax.axis_index("c")
        total = jnp.zeros((512, 256), F32)
        for ref, branch in ((ins[1], core), (ins[2], 1 - core)):
            rows = pl.ds(pl.multiple_of(branch * 192, 16), 192)
            for s in range(4):
                total = total + dot(ref[192 * s : 192 * (s + 1), :], ins[0][s, rows, :], ((0,), (0,)))
        for k in range(4):
            outs[0][z_owner(k)] = total[128 * k : 128 * (k + 1)].astype(BF16)

    return kernel_call(body, [((4, 128, 256), BF16)], [inner, mine, away], rest)[0]


def pack_factors(outers, inners):
    def body(ins, outs):
        for b in range(2):
            rows = slice(192 * b, 192 * (b + 1))
            ahead = b * (WIDE - PAD)
            parts = [ins[b][...], jnp.zeros((192, WIDE - FF - ahead), BF16)]
            if ahead:
                parts = [jnp.zeros((192, ahead), BF16), *parts]
            outs[0][rows, :WIDE] = jnp.concatenate(parts, axis=1)
            outs[0][rows, WIDE:] = ins[2 + b][...]

    return kernel_call(body, [((384, WIDE + 256), BF16)], [*outers, *inners])[0]


def gather_factors(value):
    back = turn(value, "x", 1)
    ahead = turn(value, "x", -1)
    return [value, back, turn(back[:192], "x", 1), turn(ahead[192:], "x", -1), ahead]


def after(value, rest):
    def body(ins, outs):
        outs[0][...] = ins[0][...]

    return kernel_call(body, [(value.shape, value.dtype)], [value], rest)[0]


def copies(value, rest):
    def body(ins, outs):
        for k in range(4):
            outs[0][k] = ins[0][...]

    return kernel_call(body, [((4, *value.shape), value.dtype)], [value], rest)[0]


def on_device(
    layer_input,
    rank_gate,
    rank_up,
    gate_pre,
    up_pre,
    hidden_grad,
    gate_inner,
    gate_outer,
    up_inner,
    up_outer,
):
    gate_grad, up_grad = swiglu_back(gate_pre.T, up_pre.T, hidden_grad.T)
    extra = ((0, PAD - FF), (0, 0))
    sent = jnp.concatenate((jnp.pad(gate_grad, extra), jnp.pad(up_grad, extra), layer_input.T), axis=0)
    back = turn_z(sent, 1)
    ahead = turn_z(sent, -1)
    met = [sent, back, turn_z(back, 1), ahead]
    factors = pack_factors((gate_outer, up_outer), (gate_inner.T, up_inner.T))
    factors = gather_factors(factors)
    rank = jnp.concatenate((rank_gate, rank_up), axis=1)

    grads, inputs = join(met, factors)
    away, mine, inner = hidden_sums(grads, factors)
    all_grads = lax.all_gather(grads, "x")
    mine = add(mine, lax.ppermute(away, "c", [(0, 1), (1, 0)]), [])
    rank = lax.all_gather(after(rank, [mine]), "zh")
    mine = exchange(mine.reshape(4, 192, 512), "y")
    mine = sum_blocks(mine, 0, [rank])
    rank = lax.all_gather(after(rank, [mine]), "y")
    mine = exchange(mine.reshape(4, 48, 512), "zh")
    mine = sum_blocks(mine, 4, [rank])
    mine = exchange(mine, "zh").reshape(192, 512)
    mine = exchange(copies(mine, []), "y").reshape(768, 512)
    away = lax.ppermute(mine, "c", [(0, 1), (1, 0)])

    inner_grads = jnp.sum(exchange(inner_sums(inputs, mine, away, []), "x").astype(F32), axis=0)
    input_grad = sum_blocks(exchange(input_sums(inner, mine, away, []), "zl"), 0, [])
    rank_other = lax.ppermute(rank, "c", [(0, 1), (1, 0)])
    outer_grads = outer_sums(all_grads, rank, rank_other)
    return (inner_grads[:192].T, outer_grads[0], inner_grads[192:].T, outer_grads[1], input_grad)


def solution(mesh):
    grid = Mesh(mesh.devices.reshape(4, 4, 4, 4, 2), ("x", "zl", "zh", "y", "c"))
    row = ("x", "zl")
    col = ("zh", "y", "c")
    return jax.shard_map(
        on_device,
        mesh=grid,
        in_specs=(
            P(row, col),
            P(col, row),
            P(col, row),
            P(row, col),
            P(row, col),
            P(row, col),
            P(col, row),
            P(row, col),
            P(col, row),
            P(row, col),
        ),
        out_specs=(
            P(col, row),
            P(row, col),
            P(col, row),
            P(row, col),
            P(row, col),
        ),
        check_vma=False,
    )
```

time: 387 us -> 214 us (0.55)
  the two profiles are of different devices: /device:TPU:32 before, /device:TPU:2 now
where the time goes in v2:
time: 214 us; the launch traced here: 213 us
  blocking collectives  79.7 us (37%)
  starting transfers between devices  52.9 us (25%)
  waiting for transfers between devices  38.5 us (18%)
  Pallas kernels  19.2 us (9%)
  between operations  14.3 us (7%)
  local copies, waits for them, and re-layouts  6.57 us (3%)
    all_to_all x2, blocking collectives, exchange(): return lax.all_to_all(value, axis, 0, 0)  38.7 us
    all_gather x1, blocking collectives, on_device(): rank = lax.all_gather(after(rank, [mine]), 'zh')  25.4 us
    all_to_all x4, starting transfers between devices, exchange(): return lax.all_to_all(value, axis, 0, 0)  20.2 us
    ppermute x3, waiting for transfers between devices, turn_z(): lax.ppermute(value, 'zl', [(RING[i], RING[(i + step) % 4]) for i in range...  19.5 us
    pallas_call x13, Pallas kernels, kernel_call(): pl.pallas_call(run, out_shape=[jax.ShapeDtypeStruct(shape, dtype) for sha...  19.2 us
    ppermute x4, starting transfers between devices, turn(): return lax.ppermute(value, axis, [(i, (i + step) % 4) for i in range(4)])  15.7 us
    all_gather x1, blocking collectives, on_device(): rank = lax.all_gather(after(rank, [mine]), 'y')  15.6 us
    all_to_all x4, waiting for transfers between devices, exchange(): return lax.all_to_all(value, axis, 0, 0)  14.5 us
  transfers between devices with their start and end apart: 15, of which 7 were waited for; matrix products, arithmetic and copies ran while one was open for 1% of the time, Pallas kernels for 5%

profile of v2, /device:TPU:2, one launch (start us, length us, event | category | flops | bytes accessed | tf_op | source)
XLA Modules:
  0.0 212.7 jit_solution(16190443286348360261)
XLA Ops:
  11.2 7.9 %collective-permute-start.5 = (bf16[384,1280]{1,0:T(8,128)(2,1)S(1)}, bf16[384,1280]{1,0:T(8,128)(2,1)S(1)}, u32[]{:S(2)}, u32[]{:S(2)}) collective-permute-start(bf16[384,1280]{1,0:T(8,128)(2,1)S(1)} %shard_map.137.refs_4_.refs_1_), channel_id=1, source_target_pairs={{0,384},{128,0},{256,128},{384,256},{1,385},{129,1},{257,129},{385... | collective-permute-start | bytes 2949128 | tf_op jit(solution)/shard_map/ppermute | solution.py:28
  19.1 1.9 collective-permute-start.3
  21.6 1.9 collective-permute-start
  23.5 3.9 %collective-permute-start.2 = (bf16[2112,128]{1,0:T(8,128)(2,1)S(1)}, bf16[2112,128]{1,0:T(8,128)(2,1)S(1)}, u32[]{:S(2)}, u32[]{:S(2)}) collective-permute-start(bf16[2112,128]{1,0:T(8,128)(2,1)S(1)} %fusion.4.refs_0_), channel_id=1, source_target_pairs={{0,32},{64,0},{96,64},{32,96},{1,33},{65,1},{97,65},{33,97},{2,34}... | collective-permute-start | bytes 1622024 | tf_op jit(solution)/shard_map/ppermute | solution.py:32
  27.4 8.8 %collective-permute-done.refs_1_ = bf16[2112,128]{1,0:T(8,128)(2,1)S(1)} collective-permute-done((bf16[2112,128]{1,0:T(8,128)(2,1)S(1)}, bf16[2112,128]{1,0:T(8,128)(2,1)S(1)}, u32[]{:S(2)}, u32[]{:S(2)}) %collective-permute-start) | collective-permute-done | bytes 540704 | tf_op jit(solution)/shard_map/ppermute | solution.py:32
  36.2 5.3 %collective-permute-start.1 = (bf16[2112,128]{1,0:T(8,128)(2,1)S(1)}, bf16[2112,128]{1,0:T(8,128)(2,1)S(1)}, u32[]{:S(2)}, u32[]{:S(2)}) collective-permute-start(bf16[2112,128]{1,0:T(8,128)(2,1)S(1)} %collective-permute-done.refs_1_), channel_id=1, source_target_pairs={{0,64},{64,96},{96,32},{32,0},{1,65},{65,97},{97,33},{33,1},{2,66}... | collective-permute-start | bytes 1622024 | tf_op jit(solution)/shard_map/ppermute | solution.py:32
  42.5 3.9 %collective-permute-start.6 = (bf16[192,1280]{1,0:T(8,128)(2,1)S(1)}, bf16[192,1280]{1,0:T(8,128)(2,1)S(1)}, u32[]{:S(2)}, u32[]{:S(2)}) collective-permute-start(bf16[192,1280]{1,0:T(8,128)(2,1)S(1)} %slice.17), channel_id=1, source_target_pairs={{0,384},{128,0},{256,128},{384,256},{1,385},{129,1},{257,129},{385... | collective-permute-start | bytes 1474568 | tf_op jit(solution)/shard_map/ppermute | solution.py:28
  46.5 1.9 collective-permute-start.4
  49.0 10.1 %collective-permute-done.1.refs_2_ = bf16[2112,128]{1,0:T(8,128)(2,1)S(1)} collective-permute-done((bf16[2112,128]{1,0:T(8,128)(2,1)S(1)}, bf16[2112,128]{1,0:T(8,128)(2,1)S(1)}, u32[]{:S(2)}, u32[]{:S(2)}) %collective-permute-start.1) | collective-permute-done | bytes 540704 | tf_op jit(solution)/shard_map/ppermute | solution.py:32
  60.8 4.9 %shard_map.139 = (bf16[768,512]{1,0:T(8,128)(2,1)S(1)}, bf16[768,512]{1,0:T(8,128)(2,1)S(1)}, bf16[4,384,256]{2,1,0:T(8,128)(2,1)S(1)}) custom-call(bf16[1856,512]{1,0:T(8,128)(2,1)} %get-tuple-element.13.refs_0_, bf16[384,1280]{1,0:T(8,128)(2,1)S(1)} %shard_map.137.refs_4_.refs_1_, bf16[384,1280]{1,0:T(8,128)(2,1)S(1)} %collective-permute-done.3.refs_5_.refs_2_, ...), custom_call_target="tpu_custom_call" | custom-call | flops 1000 | bytes 1000 | tf_op jit(solution)/shard_map/pallas_call | solution.py:43
  68.5 2.2 %collective-permute-done.7.refs_1_ = bf16[768,512]{1,0:T(8,128)(2,1)S(1)} collective-permute-done((bf16[768,512]{1,0:T(8,128)(2,1)S(1)}, bf16[768,512]{1,0:T(8,128)(2,1)S(1)}, u32[]{:S(2)}, u32[]{:S(2)}) %collective-permute-start.7) | collective-permute-done | bytes 786464 | tf_op jit(solution)/shard_map/ppermute | solution.py:234
  71.9 4.6 %all-to-all-start = ((bf16[4,192,512]{2,1,0:T(8,128)(2,1)}), bf16[4,192,512]{2,1,0:T(8,128)(2,1)S(1)}, u32[]{:S(2)}, u32[]{:S(2)}) async-start(bf16[4,192,512]{2,1,0:T(8,128)(2,1)} %bitcast.6), calls=%async_computation | async-start | bytes 1572864 | tf_op jit(solution)/shard_map/all_to_all | solution.py:36
  76.6 25.4 %all-gather = bf16[256,384]{1,0:T(8,128)(2,1)S(1)} all-gather(bf16[64,384]{1,0:T(8,128)(2,1)S(1)} %shard_map.141), channel_id=2, replica_groups=mesh['x'=4,'zl'=4,'zh'=4,'y'=4,'c'=2] {'zh'}, dimensions={0}, use_global_device_ids=true | all-gather | bytes 245760 | tf_op jit(solution)/shard_map/all_gather | solution.py:235
  102.7 6.6 %all-to-all-start.1 = ((bf16[4,48,512]{2,1,0:T(8,128)(2,1)}), bf16[4,48,512]{2,1,0:T(8,128)(2,1)S(1)}, u32[]{:S(2)}, u32[]{:S(2)}) async-start(bf16[4,48,512]{2,1,0:T(8,128)(2,1)} %bitcast.8), calls=%async_computation.1 | async-start | bytes 393216 | tf_op jit(solution)/shard_map/all_to_all | solution.py:36
  109.4 15.6 %all-gather.1 = bf16[16,64,384]{2,1,0:T(8,128)(2,1)S(1)} all-gather(bf16[4,64,384]{2,1,0:T(8,128)(2,1)S(1)} %shard_map.143), channel_id=3, replica_groups=mesh['x'=4,'zl'=4,'zh'=4,'y'=4,'c'=2] {'y'}, dimensions={0}, use_global_device_ids=true | all-gather | bytes 983040 | tf_op jit(solution)/shard_map/all_gather | solution.py:238
  125.0 25.7 %all_to_all.30 = bf16[4,48,512]{2,1,0:T(8,128)(2,1)S(1)} all-to-all(bf16[4,48,512]{2,1,0:T(8,128)(2,1)S(1)} %shard_map.144), channel_id=1, replica_groups=mesh['x'=4,'zl'=4,'zh'=4,'y'=4,'c'=2] {'zh'}, dimensions={0} | all-to-all | bytes 393216 | tf_op jit(solution)/shard_map/all_to_all | solution.py:36
  150.8 12.9 %all_to_all.31 = bf16[4,192,512]{2,1,0:T(8,128)(2,1)S(1)} all-to-all(bf16[4,192,512]{2,1,0:T(8,128)(2,1)S(1)} %shard_map.145), channel_id=1, replica_groups=mesh['x'=4,'zl'=4,'zh'=4,'y'=4,'c'=2] {'y'}, dimensions={0} | all-to-all | bytes 1572864 | tf_op jit(solution)/shard_map/all_to_all | solution.py:36
  165.7 2.3 %collective-permute-done.8.refs_2_ = bf16[768,512]{1,0:T(8,128)(2,1)S(1)} collective-permute-done((bf16[768,512]{1,0:T(8,128)(2,1)S(1)}, bf16[768,512]{1,0:T(8,128)(2,1)S(1)}, u32[]{:S(2)}, u32[]{:S(2)}) %collective-permute-start.8) | collective-permute-done | bytes 786464 | tf_op jit(solution)/shard_map/ppermute | solution.py:243
  169.7 5.6 %all-to-all-start.4 = ((bf16[4,384,256]{2,1,0:T(8,128)(2,1)}), bf16[4,384,256]{2,1,0:T(8,128)(2,1)}, u32[]{:S(2)}, u32[]{:S(2)}) async-start(bf16[4,384,256]{2,1,0:T(8,128)(2,1)} %shard_map.146), calls=%async_computation.4 | async-start | bytes 1572864 | tf_op jit(solution)/shard_map/all_to_all | solution.py:36
  176.7 10.0 %all-to-all-done.4 = bf16[4,384,256]{2,1,0:T(8,128)(2,1)} async-done(((bf16[4,384,256]{2,1,0:T(8,128)(2,1)}), bf16[4,384,256]{2,1,0:T(8,128)(2,1)}, u32[]{:S(2)}, u32[]{:S(2)}) %all-to-all-start.4) | async-done | bytes 786464 | tf_op jit(solution)/shard_map/all_to_all | solution.py:36
  186.7 3.4 %all-to-all-start.5 = ((bf16[4,128,256]{2,1,0:T(8,128)(2,1)}), bf16[4,128,256]{2,1,0:T(8,128)(2,1)S(1)}, u32[]{:S(2)}, u32[]{:S(2)}) async-start(bf16[4,128,256]{2,1,0:T(8,128)(2,1)} %shard_map.148), calls=%async_computation.5 | async-start | bytes 524288 | tf_op jit(solution)/shard_map/all_to_all | solution.py:36
  190.1 1.9 collective-permute-start.9
  194.1 4.5 %all-to-all-done.5.refs_0_ = bf16[4,128,256]{2,1,0:T(8,128)(2,1)S(1)} async-done(((bf16[4,128,256]{2,1,0:T(8,128)(2,1)}), bf16[4,128,256]{2,1,0:T(8,128)(2,1)S(1)}, u32[]{:S(2)}, u32[]{:S(2)}) %all-to-all-start.5) | async-done | bytes 262176 | tf_op jit(solution)/shard_map/all_to_all | solution.py:36
  199.3 6.6 %shard_map.147 = (f32[192,924]{1,0:T(8,128)}, f32[192,924]{1,0:T(8,128)}) custom-call(bf16[4,1856,512]{2,1,0:T(8,128)(2,1)} %bitcast.58, bf16[4,4,64,384]{3,2,1,0:T(8,128)(2,1)S(1)} %bitcast.49, bf16[4,4,64,384]{3,2,1,0:T(8,128)(2,1)S(1)} %collective-permute-done.9.refs_2_), custom_call_target="tpu_custom_call" | custom-call | flops 1000 | bytes 1000 | tf_op jit(solution)/shard_map/pallas_call | solution.py:43
  (58 shorter events, 20.4 us)
Async XLA Ops:
  7.2 192.2 %all-gather.5.cloned.1.call-start = ((), (), s32[]{:S(2)}) async-start(), calls=%async_computation.6 | async-start | bytes 9502720 | tf_op jit(solution)/shard_map/all_gather | solution.py:233
  7.2 1.0 copy-start.2
  8.2 1.0 copy-start.3
  11.0 10.1 %copy-start.7 = (bf16[128,924]{0,1:T(8,128)(2,1)S(1)}, bf16[128,924]{0,1:T(8,128)(2,1)}, u32[]{:S(2)}) copy-start(bf16[128,924]{0,1:T(8,128)(2,1)} %param.13) | copy-start | bytes 709636
  11.0 10.1 %copy-start.8 = (bf16[128,924]{0,1:T(8,128)(2,1)S(1)}, bf16[128,924]{0,1:T(8,128)(2,1)}, u32[]{:S(2)}) copy-start(bf16[128,924]{0,1:T(8,128)(2,1)} %param.15) | copy-start | bytes 709636
  11.0 10.1 %copy-start.9 = (bf16[128,924]{0,1:T(8,128)(2,1)S(1)}, bf16[128,924]{0,1:T(8,128)(2,1)}, u32[]{:S(2)}) copy-start(bf16[128,924]{0,1:T(8,128)(2,1)} %param.14) | copy-start | bytes 709636
  11.2 10.2 %copy-start.10 = (bf16[128,256]{1,0:T(8,128)(2,1)S(1)}, bf16[128,256]{1,0:T(8,128)(2,1)}, u32[]{:S(2)}) copy-start(bf16[128,256]{1,0:T(8,128)(2,1)} %param.10) | copy-start | bytes 196612
  11.2 30.3 %collective-permute-start.5 = (bf16[384,1280]{1,0:T(8,128)(2,1)S(1)}, bf16[384,1280]{1,0:T(8,128)(2,1)S(1)}, u32[]{:S(2)}, u32[]{:S(2)}) collective-permute-start(bf16[384,1280]{1,0:T(8,128)(2,1)S(1)} %shard_map.137.refs_4_.refs_1_), channel_id=1, source_target_pairs={{0,384},{128,0},{256,128},{384,256},{1,385},{129,1},{257,129},{385... | collective-permute-start | bytes 2949128 | tf_op jit(solution)/shard_map/ppermute | solution.py:28
  19.1 27.3 %collective-permute-start.3 = (bf16[384,1280]{1,0:T(8,128)(2,1)S(1)}, bf16[384,1280]{1,0:T(8,128)(2,1)S(1)}, u32[]{:S(2)}, u32[]{:S(2)}) collective-permute-start(bf16[384,1280]{1,0:T(8,128)(2,1)S(1)} %shard_map.137.refs_4_.refs_1_), channel_id=1, source_target_pairs={{0,128},{128,256},{256,384},{384,0},{1,129},{129,257},{257,385},{3... | collective-permute-start | bytes 2949128 | tf_op jit(solution)/shard_map/ppermute | solution.py:28
  21.6 14.7 %collective-permute-start = (bf16[2112,128]{1,0:T(8,128)(2,1)S(1)}, bf16[2112,128]{1,0:T(8,128)(2,1)S(1)}, u32[]{:S(2)}, u32[]{:S(2)}) collective-permute-start(bf16[2112,128]{1,0:T(8,128)(2,1)S(1)} %fusion.4.refs_0_), channel_id=1, source_target_pairs={{0,64},{64,96},{96,32},{32,0},{1,65},{65,97},{97,33},{33,1},{2,66}... | collective-permute-start | bytes 1622024 | tf_op jit(solution)/shard_map/ppermute | solution.py:32
  23.5 25.5 %collective-permute-start.2 = (bf16[2112,128]{1,0:T(8,128)(2,1)S(1)}, bf16[2112,128]{1,0:T(8,128)(2,1)S(1)}, u32[]{:S(2)}, u32[]{:S(2)}) collective-permute-start(bf16[2112,128]{1,0:T(8,128)(2,1)S(1)} %fusion.4.refs_0_), channel_id=1, source_target_pairs={{0,32},{64,0},{96,64},{32,96},{1,33},{65,1},{97,65},{33,97},{2,34}... | collective-permute-start | bytes 1622024 | tf_op jit(solution)/shard_map/ppermute | solution.py:32
  36.2 22.8 %collective-permute-start.1 = (bf16[2112,128]{1,0:T(8,128)(2,1)S(1)}, bf16[2112,128]{1,0:T(8,128)(2,1)S(1)}, u32[]{:S(2)}, u32[]{:S(2)}) collective-permute-start(bf16[2112,128]{1,0:T(8,128)(2,1)S(1)} %collective-permute-done.refs_1_), channel_id=1, source_target_pairs={{0,64},{64,96},{96,32},{32,0},{1,65},{65,97},{97,33},{33,1},{2,66}... | collective-permute-start | bytes 1622024 | tf_op jit(solution)/shard_map/ppermute | solution.py:32
  42.5 16.6 %collective-permute-start.6 = (bf16[192,1280]{1,0:T(8,128)(2,1)S(1)}, bf16[192,1280]{1,0:T(8,128)(2,1)S(1)}, u32[]{:S(2)}, u32[]{:S(2)}) collective-permute-start(bf16[192,1280]{1,0:T(8,128)(2,1)S(1)} %slice.17), channel_id=1, source_target_pairs={{0,384},{128,0},{256,128},{384,256},{1,385},{129,1},{257,129},{385... | collective-permute-start | bytes 1474568 | tf_op jit(solution)/shard_map/ppermute | solution.py:28
  46.5 12.6 %collective-permute-start.4 = (bf16[192,1280]{1,0:T(8,128)(2,1)S(1)}, bf16[192,1280]{1,0:T(8,128)(2,1)S(1)}, u32[]{:S(2)}, u32[]{:S(2)}) collective-permute-start(bf16[192,1280]{1,0:T(8,128)(2,1)S(1)} %slice.16), channel_id=1, source_target_pairs={{0,128},{128,256},{256,384},{384,0},{1,129},{129,257},{257,385},{3... | collective-permute-start | bytes 1474568 | tf_op jit(solution)/shard_map/ppermute | solution.py:28
  66.6 4.2 %collective-permute-start.7 = (bf16[768,512]{1,0:T(8,128)(2,1)S(1)}, bf16[768,512]{1,0:T(8,128)(2,1)S(1)}, u32[]{:S(2)}, u32[]{:S(2)}) collective-permute-start(bf16[768,512]{1,0:T(8,128)(2,1)S(1)} %get-tuple-element.15), channel_id=1, source_target_pairs={{0,1},{1,0},{2,3},{3,2},{4,5},{5,4},{6,7},{7,6},{8,9},{9,8},{10,11... | collective-permute-start | bytes 2359304 | tf_op jit(solution)/shard_map/ppermute | solution.py:234
  71.9 4.6 %copy-start.11 = (bf16[64,192]{1,0:T(8,128)(2,1)S(1)}, bf16[64,192]{1,0:T(8,128)(2,1)}, u32[]{:S(2)}) copy-start(bf16[64,192]{1,0:T(8,128)(2,1)} %param.12) | copy-start | bytes 73732
  71.9 4.6 %copy-start.12 = (bf16[64,192]{1,0:T(8,128)(2,1)S(1)}, bf16[64,192]{1,0:T(8,128)(2,1)}, u32[]{:S(2)}) copy-start(bf16[64,192]{1,0:T(8,128)(2,1)} %param.11) | copy-start | bytes 73732
  71.9 30.1 %all-to-all-start = ((bf16[4,192,512]{2,1,0:T(8,128)(2,1)}), bf16[4,192,512]{2,1,0:T(8,128)(2,1)S(1)}, u32[]{:S(2)}, u32[]{:S(2)}) async-start(bf16[4,192,512]{2,1,0:T(8,128)(2,1)} %bitcast.6), calls=%async_computation | async-start | bytes 1572864 | tf_op jit(solution)/shard_map/all_to_all | solution.py:36
  102.7 22.3 %all-to-all-start.1 = ((bf16[4,48,512]{2,1,0:T(8,128)(2,1)}), bf16[4,48,512]{2,1,0:T(8,128)(2,1)S(1)}, u32[]{:S(2)}, u32[]{:S(2)}) async-start(bf16[4,48,512]{2,1,0:T(8,128)(2,1)} %bitcast.8), calls=%async_computation.1 | async-start | bytes 393216 | tf_op jit(solution)/shard_map/all_to_all | solution.py:36
  163.8 4.2 %collective-permute-start.8 = (bf16[768,512]{1,0:T(8,128)(2,1)S(1)}, bf16[768,512]{1,0:T(8,128)(2,1)S(1)}, u32[]{:S(2)}, u32[]{:S(2)}) collective-permute-start(bf16[768,512]{1,0:T(8,128)(2,1)S(1)} %bitcast.50), channel_id=1, source_target_pairs={{0,1},{1,0},{2,3},{3,2},{4,5},{5,4},{6,7},{7,6},{8,9},{9,8},{10,11... | collective-permute-start | bytes 2359304 | tf_op jit(solution)/shard_map/ppermute | solution.py:243
  169.7 5.6 %copy-start.1 = (bf16[4,384,256]{2,1,0:T(8,128)(2,1)S(1)}, bf16[4,384,256]{2,1,0:T(8,128)(2,1)}, u32[]{:S(2)}) copy-start(bf16[4,384,256]{2,1,0:T(8,128)(2,1)} %copy-done) | copy-start | bytes 2359300
  169.7 17.1 %all-to-all-start.4 = ((bf16[4,384,256]{2,1,0:T(8,128)(2,1)}), bf16[4,384,256]{2,1,0:T(8,128)(2,1)}, u32[]{:S(2)}, u32[]{:S(2)}) async-start(bf16[4,384,256]{2,1,0:T(8,128)(2,1)} %shard_map.146), calls=%async_computation.4 | async-start | bytes 1572864 | tf_op jit(solution)/shard_map/all_to_all | solution.py:36
  186.7 11.9 %all-to-all-start.5 = ((bf16[4,128,256]{2,1,0:T(8,128)(2,1)}), bf16[4,128,256]{2,1,0:T(8,128)(2,1)S(1)}, u32[]{:S(2)}, u32[]{:S(2)}) async-start(bf16[4,128,256]{2,1,0:T(8,128)(2,1)} %shard_map.148), calls=%async_computation.5 | async-start | bytes 524288 | tf_op jit(solution)/shard_map/all_to_all | solution.py:36
  190.1 9.2 %collective-permute-start.9 = (bf16[4,4,64,384]{3,2,1,0:T(8,128)(2,1)S(1)}, bf16[4,4,64,384]{3,2,1,0:T(8,128)(2,1)S(1)}, u32[]{:S(2)}, u32[]{:S(2)}) collective-permute-start(bf16[4,4,64,384]{3,2,1,0:T(8,128)(2,1)S(1)} %bitcast.48), channel_id=1, source_target_pairs={{0,1},{1,0},{2,3},{3,2},{4,5},{5,4},{6,7},{7,6},{8,9},{9,8},{10,11... | collective-permute-start | bytes 2359304 | tf_op jit(solution)/shard_map/ppermute | solution.py:247
  (4 other events, 3.6 us)
Sparse Core Ops, SparseCore 0:
  60.9 87.9 all-gather.4

commit v3 on v2

v3 whole, which is shorter than its diff:
```python
import jax
import jax.numpy as jnp
from jax import lax
from jax.experimental import pallas as pl
from jax.experimental.pallas import tpu as pltpu
from jax.sharding import Mesh
from jax.sharding import PartitionSpec as P

F32 = jnp.float32
BF16 = jnp.bfloat16
RING = (0, 2, 3, 1)
FF = 924
PAD = 928
WIDE = 1024


def swiglu_back(gate_pre, up_pre, hidden_grad):
    gate_val = gate_pre.astype(F32)
    up_val = up_pre.astype(F32)
    grad_val = hidden_grad.astype(F32)
    logistic = jax.nn.sigmoid(gate_val)
    gate_grad = (grad_val * up_val * logistic * (1.0 + gate_val * (1.0 - logistic))).astype(BF16)
    up_grad = (grad_val * gate_val * logistic).astype(BF16)
    return (gate_grad, up_grad)


def turn(value, axis, step):
    return lax.ppermute(value, axis, [(i, (i + step) % 4) for i in range(4)])


def turn_z(value, step):
    return lax.ppermute(value, "zl", [(RING[i], RING[(i + step) % 4]) for i in range(4)])


def exchange(value, axis):
    return lax.all_to_all(value, axis, 0, 0)


def kernel_call(body, out, vmem, rest=(), near=(), limit=48):
    held = [*vmem, *near]

    def run(*refs):
        body(refs[: len(vmem)], refs[len(held) + len(rest) :])

    return pl.pallas_call(
        run,
        out_shape=[jax.ShapeDtypeStruct(shape, dtype) for shape, dtype in out],
        in_specs=[pl.BlockSpec(memory_space=pltpu.VMEM)] * len(held)
        + [pl.BlockSpec(memory_space=pl.ANY)] * len(rest),
        out_specs=[pl.BlockSpec(memory_space=pltpu.VMEM)] * len(out),
        compiler_params=pltpu.CompilerParams(vmem_limit_bytes=limit * 2**20),
        cost_estimate=pl.CostEstimate(flops=1000, bytes_accessed=1000, transcendentals=0),
    )(*held, *rest)


def dot(left, right, dims):
    return lax.dot_general(left, right, (dims, ((), ())), preferred_element_type=F32)


def z_owner(k):
    line = lax.axis_index("zl")
    spot = jnp.where(line == 0, 0, jnp.where(line == 1, 3, line - 1))
    place = (spot - k + 4) % 4
    return jnp.where(place == 0, 0, jnp.where(place == 3, 1, place + 1))


def copy_call(copies, out, scratch, arrays, rest, body=None, limit=48):
    n_in = len(arrays) + len(rest)

    def run(*refs):
        outs, held, sems = refs[n_in : n_in + len(out)], refs[n_in + len(out) : -1], refs[-1]
        pairs = copies(refs[: len(arrays)], outs, held)
        made = [pltpu.make_async_copy(source, target, sems.at[k]) for k, (source, target) in enumerate(pairs)]
        for copy in made:
            copy.start()
        if body is None:
            for copy in made:
                copy.wait()
        else:
            body(made, outs, *held)

    place = pl.ANY if body is None else pltpu.VMEM
    return pl.pallas_call(
        run,
        out_shape=[jax.ShapeDtypeStruct(shape, BF16) for shape in out],
        in_specs=[pl.BlockSpec(memory_space=pl.ANY)] * n_in,
        out_specs=[pl.BlockSpec(memory_space=place)] * len(out),
        scratch_shapes=[*scratch, pltpu.SemaphoreType.DMA((16,))],
        compiler_params=pltpu.CompilerParams(vmem_limit_bytes=limit * 2**20),
        cost_estimate=pl.CostEstimate(flops=1000, bytes_accessed=1000, transcendentals=0),
    )(*arrays, *rest)


def factor_rows(refs, s, rows, half, columns):
    if s == 2:
        return refs[2 + half].at[:, columns]
    return refs[{0: 0, 1: 1, 3: 4}[s]].at[rows, columns]


def hidden_sums(met, factors, branch, rest):
    def copies(ins, outs, held):
        grad_ref, outer_ref = held
        b = branch(lax.axis_index("c"))
        rows = pl.ds(pl.multiple_of(b * (2 * PAD - WIDE), 16), WIDE)
        pairs = [(ins[k].at[rows, :], grad_ref.at[:, 128 * k : 128 * (k + 1)]) for k in range(4)]
        rows = pl.ds(pl.multiple_of(b * 192, 16), 192)
        sources = [ins[4 + k].at[:, :WIDE] if k in (2, 3) else ins[4 + k].at[rows, :WIDE] for k in range(5)]
        return pairs + [(source, outer_ref.at[s]) for s, source in enumerate(sources)]

    def body(made, outs, grad_ref, outer_ref):
        for copy in made[:4]:
            copy.wait()
        for s, place in ((0, 0), (1, 1), (3, 4), (2, 2 + branch(lax.axis_index("c")))):
            for copy in {0: made[4:5], 1: made[5:6], 2: made[6:8], 3: made[8:9]}[s]:
                copy.wait()
            part = dot(outer_ref[place], grad_ref[...], ((1,), (0,)))
            outs[0][192 * s : 192 * (s + 1), :] = part.astype(BF16)

    scratch = [pltpu.VMEM((WIDE, 512), BF16), pltpu.VMEM((5, 192, WIDE), BF16)]
    return copy_call(copies, [(768, 512)], scratch, [*met, *factors], rest, body)[0]


def join(met, rest):
    def copies(ins, outs, held):
        return [(ins[k].at[: 2 * PAD, :], outs[0].at[:, 128 * k : 128 * (k + 1)]) for k in range(4)]

    return copy_call(copies, [(2 * PAD, 512)], [], met, rest)[0]


def join_inner(met, factors, rest):
    def copies(ins, outs, held):
        pairs = [(ins[k].at[2 * PAD :, :], outs[0].at[:, 128 * k : 128 * (k + 1)]) for k in range(4)]
        columns = slice(WIDE, WIDE + 256)
        for s in range(4):
            for b in range(2):
                rows = slice(192 * b, 192 * (b + 1))
                pairs.append((factor_rows(ins[4:], s, rows, b, columns), outs[1].at[s, rows, :]))
        return pairs

    return copy_call(copies, [(256, 512), (4, 384, 256)], [], [*met, *factors], rest)


def add(left, right, rest):
    def body(ins, outs):
        outs[0][...] = (ins[0][...].astype(F32) + ins[1][...].astype(F32)).astype(BF16)

    return kernel_call(body, [(left.shape, BF16)], [left, right], rest)[0]


def sum_blocks(value, copies, rest, near):
    shape = value.shape[1:]

    def body(ins, outs):
        total = (ins[0][0].astype(F32) + ins[0][1].astype(F32)) + (ins[0][2].astype(F32) + ins[0][3].astype(F32))
        for k in range(copies):
            outs[0][k] = total.astype(BF16)

    return kernel_call(body, [((copies, *shape), BF16)], [value], rest, near)[0]


def outer_sums(grads, rank, other, rest):
    def body(ins, outs):
        first = lax.axis_index("c") == 0
        totals = [0.0, 0.0]
        for x in range(4):
            pieces = []
            for k in range(4):
                spot = (z_owner(k), x)
                mine, away = ins[1][spot], ins[2][spot]
                pieces.append(jnp.where(first, mine, away))
                pieces.append(jnp.where(first, away, mine))
            rank_rows = jnp.concatenate(pieces, axis=0)
            for b in range(2):
                left = rank_rows[:, 192 * b : 192 * (b + 1)]
                part = dot(left, ins[0][x, PAD * b : PAD * (b + 1), :], ((0,), (1,)))
                totals[b] = totals[b] + part
        for b in range(2):
            outs[b][...] = totals[b][:, :FF]
        outs[2][...] = jnp.zeros((8, 128), F32)

    return kernel_call(body, [((192, FF), F32)] * 2 + [((8, 128), F32)], [grads, rank, other], rest)


def inner_total(value, rest):
    def body(ins, outs):
        for b in range(2):
            rows = slice(192 * b, 192 * (b + 1))
            low = ins[0][0, rows, :].astype(F32) + ins[0][1, rows, :].astype(F32)
            outs[b][...] = low + (ins[0][2, rows, :].astype(F32) + ins[0][3, rows, :].astype(F32))

    return kernel_call(body, [((192, 256), F32)] * 2, [value], rest)


def last_sums(inputs, inner, mine, away):
    def body(ins, outs):
        core = lax.axis_index("c")
        me = lax.axis_index("x")
        total = jnp.zeros((512, 256), F32)
        for ref, branch in ((ins[2], core), (ins[3], 1 - core)):
            rows = pl.ds(pl.multiple_of(branch * 192, 16), 192)
            for s in range(4):
                grad = ref[192 * s : 192 * (s + 1), :]
                outs[0][(me - s + 4) % 4, rows, :] = dot(grad, ins[0][...], ((1,), (1,))).astype(BF16)
                total = total + dot(grad, ins[1][s, rows, :], ((0,), (0,)))
        for k in range(4):
            outs[1 + k][...] = total[128 * k : 128 * (k + 1)].astype(outs[1 + k].dtype)

    out = [((4, 384, 256), BF16), ((128, 256), F32)] + [((128, 256), BF16)] * 3
    return kernel_call(body, out, [inputs, inner, mine, away])


def input_total(parts, rest):
    def body(ins, outs):
        total = ins[0][...] + ins[1][...].astype(F32)
        outs[0][...] = (total + (ins[2][...].astype(F32) + ins[3][...].astype(F32))).astype(BF16)

    return kernel_call(body, [((128, 256), BF16)], parts, rest)[0]


def pack_factors(outers, inners, rest):
    def body(ins, outs):
        for b in range(2):
            rows = slice(192 * b, 192 * (b + 1))
            ahead = b * (WIDE - PAD)
            parts = [ins[b][...], jnp.zeros((192, WIDE - FF - ahead), BF16)]
            if ahead:
                parts = [jnp.zeros((192, ahead), BF16), *parts]
            outs[0][rows, :WIDE] = jnp.concatenate(parts, axis=1)
            outs[0][rows, WIDE:] = ins[2 + b][...]

    return kernel_call(body, [((384, WIDE + 256), BF16)], [*outers, *inners], rest)[0]


def gather_factors(value):
    back = turn(value, "x", 1)
    ahead = turn(value, "x", -1)
    return [value, back, turn(back[:192], "x", 1), turn(ahead[192:], "x", -1), ahead]


def after(value, rest):
    def body(ins, outs):
        outs[0][...] = ins[0][...]

    return kernel_call(body, [(value.shape, value.dtype)], [value], rest)[0]


def on_device(
    layer_input,
    rank_gate,
    rank_up,
    gate_pre,
    up_pre,
    hidden_grad,
    gate_inner,
    gate_outer,
    up_inner,
    up_outer,
):
    gate_grad, up_grad = swiglu_back(gate_pre.T, up_pre.T, hidden_grad.T)
    extra = ((0, PAD - FF), (0, 0))
    sent = jnp.concatenate((jnp.pad(gate_grad, extra), jnp.pad(up_grad, extra), layer_input.T), axis=0)
    back = turn_z(sent, 1)
    ahead = turn_z(sent, -1)
    met = [sent, back, turn_z(back, 1), ahead]
    factors = pack_factors((gate_outer, up_outer), (gate_inner.T, up_inner.T), [sent])
    factors = gather_factors(factors)
    rank = jnp.concatenate((rank_gate, rank_up), axis=1)

    away = hidden_sums(met, factors, lambda core: 1 - core, [])
    grads = join(met, [away])
    all_grads = lax.all_gather(grads, "x")
    mine = hidden_sums(met, factors, lambda core: core, [grads])
    mine = add(mine, lax.ppermute(away, "c", [(0, 1), (1, 0)]), [])
    rank = lax.all_gather(after(rank, [mine]), "zh")
    mine = exchange(mine.reshape(4, 192, 512), "y")
    mine = sum_blocks(mine, 4, [], [rank])
    inputs, inner = join_inner(met, factors, [mine])
    rank = lax.all_gather(after(rank, [mine]), "y")
    rank_other = lax.ppermute(rank, "c", [(0, 1), (1, 0)])
    mine = exchange(mine, "zh")
    mine = sum_blocks(mine, 4, [], [rank_other, inputs])
    *outer_grads, token = outer_sums(all_grads, rank, rank_other, [mine])
    mine = after(exchange(mine, "y").reshape(768, 512), [token])
    away = lax.ppermute(mine, "c", [(0, 1), (1, 0)])

    inner_grads, *input_parts = last_sums(inputs, inner, mine, away)
    inner_grads = inner_total(exchange(inner_grads, "x"), [])
    input_grad = input_total([input_parts[0]] + [turn_z(input_parts[s], -s) for s in (1, 2, 3)], [])
    return (inner_grads[0].T, outer_grads[0], inner_grads[1].T, outer_grads[1], input_grad)


def solution(mesh):
    grid = Mesh(mesh.devices.reshape(4, 4, 4, 4, 2), ("x", "zl", "zh", "y", "c"))
    row = ("x", "zl")
    col = ("zh", "y", "c")
    return jax.shard_map(
        on_device,
        mesh=grid,
        in_specs=(
            P(row, col),
            P(col, row),
            P(col, row),
            P(row, col),
            P(row, col),
            P(row, col),
            P(col, row),
            P(row, col),
            P(col, row),
            P(row, col),
        ),
        out_specs=(
            P(col, row),
            P(row, col),
            P(col, row),
            P(row, col),
            P(row, col),
        ),
        check_vma=False,
    )
```

time: 214 us -> 199 us (0.930)
  blocking collectives: 79.7 us -> 40.2 us
  starting transfers between devices: 52.9 us -> 68.2 us
  waiting for transfers between devices: 38.5 us -> 43.6 us
  Pallas kernels: 19.2 us -> 21.8 us
    all_to_all x2 -> x0, blocking collectives: 38.7 us -> none  [exchange(): return lax.all_to_all(value, axis, 0, 0)]
    ppermute x3 -> x6, starting transfers between devices: 11.1 us -> 21.6 us  [turn_z(): lax.ppermute(value, 'zl', [(RING[i], RING[(i + step) % 4]) for i in range...]
    pallas_call x0 -> x4, Pallas kernels: none -> 7.2 us  [copy_call(): pl.pallas_call(run, out_shape=[jax.ShapeDtypeStruct(shape, BF16) for shap...]
    all_to_all x4, waiting for transfers between devices: 14.5 us -> 19.9 us  [exchange(): return lax.all_to_all(value, axis, 0, 0)]
    pallas_call x13 -> x11, Pallas kernels: 19.2 us -> 14.6 us  [kernel_call(): pl.pallas_call(run, out_shape=[jax.ShapeDtypeStruct(shape, dtype) for sha...]
    all_to_all x4, starting transfers between devices: 20.2 us -> 24 us  [exchange(): return lax.all_to_all(value, axis, 0, 0)]
    ppermute x1, waiting for transfers between devices: 2.24 us -> 0.01 us  [on_device(): mine = add(mine, lax.ppermute(away, 'c', [(0, 1), (1, 0)]), [])]
    unnamed x27 -> x51, local copies, waits for them, and re-layouts: 5.73 us -> 7.93 us
  transfers between devices with their start and end apart: 15 -> 18, of which waited for: 7 -> 7; matrix products, arithmetic and copies ran while one was open for 1% -> 0% of each run, Pallas kernels for 5% -> 8%
where the time goes in v3:
time: 199 us; the launch traced here: 198 us
  starting transfers between devices  68.2 us (34%)
  waiting for transfers between devices  43.6 us (22%)
  blocking collectives  40.2 us (20%)
  Pallas kernels  21.8 us (11%)
  between operations  14.5 us (7%)
  local copies, waits for them, and re-layouts  8 us (4%)
    all_gather x1, blocking collectives, on_device(): rank = lax.all_gather(after(rank, [mine]), 'zh')  26.1 us
    all_to_all x4, starting transfers between devices, exchange(): return lax.all_to_all(value, axis, 0, 0)  24 us
    ppermute x6, starting transfers between devices, turn_z(): lax.ppermute(value, 'zl', [(RING[i], RING[(i + step) % 4]) for i in range...  21.6 us
    ppermute x6, waiting for transfers between devices, turn_z(): lax.ppermute(value, 'zl', [(RING[i], RING[(i + step) % 4]) for i in range...  21.4 us
    all_to_all x4, waiting for transfers between devices, exchange(): return lax.all_to_all(value, axis, 0, 0)  19.9 us
    ppermute x4, starting transfers between devices, turn(): return lax.ppermute(value, axis, [(i, (i + step) % 4) for i in range(4)])  16.8 us
    pallas_call x11, Pallas kernels, kernel_call(): pl.pallas_call(run, out_shape=[jax.ShapeDtypeStruct(shape, dtype) for sha...  14.6 us
    all_gather x1, blocking collectives, on_device(): rank = lax.all_gather(after(rank, [mine]), 'y')  14.1 us
  transfers between devices with their start and end apart: 18, of which 7 were waited for; matrix products, arithmetic and copies ran while one was open for 0% of the time, Pallas kernels for 8%

profile of v3, /device:TPU:2, one launch (start us, length us, event | category | flops | bytes accessed | tf_op | source)
XLA Modules:
  0.0 197.9 jit_solution(12433862046884249221)
XLA Ops:
  10.0 3.4 %collective-permute-start.3 = (bf16[384,1280]{1,0:T(8,128)(2,1)S(1)}, bf16[384,1280]{1,0:T(8,128)(2,1)S(1)}, u32[]{:S(2)}, u32[]{:S(2)}) collective-permute-start(bf16[384,1280]{1,0:T(8,128)(2,1)S(1)} %shard_map.137.refs_4_), channel_id=1, source_target_pairs={{0,128},{128,256},{256,384},{384,0},{1,129},{129,257},{257,385},{3... | collective-permute-start | bytes 2949128 | tf_op jit(solution)/shard_map/ppermute | solution.py:28
  13.4 6.3 %collective-permute-start.5 = (bf16[384,1280]{1,0:T(8,128)(2,1)S(1)}, bf16[384,1280]{1,0:T(8,128)(2,1)S(1)}, u32[]{:S(2)}, u32[]{:S(2)}) collective-permute-start(bf16[384,1280]{1,0:T(8,128)(2,1)S(1)} %shard_map.137.refs_4_), channel_id=1, source_target_pairs={{0,384},{128,0},{256,128},{384,256},{1,385},{129,1},{257,129},{385... | collective-permute-start | bytes 2949128 | tf_op jit(solution)/shard_map/ppermute | solution.py:28
  21.7 3.9 %collective-permute-start.2 = (bf16[2112,128]{1,0:T(8,128)(2,1)S(1)}, bf16[2112,128]{1,0:T(8,128)(2,1)S(1)}, u32[]{:S(2)}, u32[]{:S(2)}) collective-permute-start(bf16[2112,128]{1,0:T(8,128)(2,1)S(1)} %fusion.4.refs_4_.refs_0_), channel_id=1, source_target_pairs={{0,32},{64,0},{96,64},{32,96},{1,33},{65,1},{97,65},{33,97},{2,34}... | collective-permute-start | bytes 1622024 | tf_op jit(solution)/shard_map/ppermute | solution.py:32
  25.6 8.8 %collective-permute-done.refs_1_ = bf16[2112,128]{1,0:T(8,128)(2,1)S(1)} collective-permute-done((bf16[2112,128]{1,0:T(8,128)(2,1)S(1)}, bf16[2112,128]{1,0:T(8,128)(2,1)S(1)}, u32[]{:S(2)}, u32[]{:S(2)}) %collective-permute-start) | collective-permute-done | bytes 540704 | tf_op jit(solution)/shard_map/ppermute | solution.py:32
  34.4 5.3 %collective-permute-start.1 = (bf16[2112,128]{1,0:T(8,128)(2,1)S(1)}, bf16[2112,128]{1,0:T(8,128)(2,1)S(1)}, u32[]{:S(2)}, u32[]{:S(2)}) collective-permute-start(bf16[2112,128]{1,0:T(8,128)(2,1)S(1)} %collective-permute-done.refs_1_), channel_id=1, source_target_pairs={{0,64},{64,96},{96,32},{32,0},{1,65},{65,97},{97,33},{33,1},{2,66}... | collective-permute-start | bytes 1622024 | tf_op jit(solution)/shard_map/ppermute | solution.py:32
  39.8 2.8 %collective-permute-start.4 = (bf16[192,1280]{1,0:T(8,128)(2,1)S(1)}, bf16[192,1280]{1,0:T(8,128)(2,1)S(1)}, u32[]{:S(2)}, u32[]{:S(2)}) collective-permute-start(bf16[192,1280]{1,0:T(8,128)(2,1)S(1)} %slice.8), channel_id=1, source_target_pairs={{0,128},{128,256},{256,384},{384,0},{1,129},{129,257},{257,385},{3... | collective-permute-start | bytes 1474568 | tf_op jit(solution)/shard_map/ppermute | solution.py:28
  42.6 4.3 %collective-permute-start.6 = (bf16[192,1280]{1,0:T(8,128)(2,1)S(1)}, bf16[192,1280]{1,0:T(8,128)(2,1)S(1)}, u32[]{:S(2)}, u32[]{:S(2)}) collective-permute-start(bf16[192,1280]{1,0:T(8,128)(2,1)S(1)} %slice.9), channel_id=1, source_target_pairs={{0,384},{128,0},{256,128},{384,256},{1,385},{129,1},{257,129},{385... | collective-permute-start | bytes 1474568 | tf_op jit(solution)/shard_map/ppermute | solution.py:28
  47.2 10.1 %collective-permute-done.1.refs_2_ = bf16[2112,128]{1,0:T(8,128)(2,1)S(1)} collective-permute-done((bf16[2112,128]{1,0:T(8,128)(2,1)S(1)}, bf16[2112,128]{1,0:T(8,128)(2,1)S(1)}, u32[]{:S(2)}, u32[]{:S(2)}) %collective-permute-start.1) | collective-permute-done | bytes 540704 | tf_op jit(solution)/shard_map/ppermute | solution.py:32
  57.3 2.2 %shard_map.138.refs_4_ = bf16[768,512]{1,0:T(8,128)(2,1)S(1)} custom-call(bf16[2112,128]{1,0:T(8,128)(2,1)S(1)} %fusion.4.refs_4_.refs_0_, bf16[2112,128]{1,0:T(8,128)(2,1)S(1)} %collective-permute-done.refs_1_, bf16[2112,128]{1,0:T(8,128)(2,1)S(1)} %collective-permute-done.1.refs_2_, bf16[2112,128]{1,0:T(8,128)(2,1)S(1)} %collective-permute-done.2.refs_3_, ...), custom_call_target="tpu_custom_call" | custom-call | flops 1000 | bytes 1000 | tf_op jit(solution)/shard_map/pallas_call | solution.py:83
  67.0 2.2 %shard_map.140.refs_0_ = bf16[768,512]{1,0:T(8,128)(2,1)S(1)} custom-call(bf16[2112,128]{1,0:T(8,128)(2,1)S(1)} %fusion.4.refs_4_.refs_0_, bf16[2112,128]{1,0:T(8,128)(2,1)S(1)} %collective-permute-done.refs_1_, bf16[2112,128]{1,0:T(8,128)(2,1)S(1)} %copy-done.5, bf16[2112,128]{1,0:T(8,128)(2,1)S(1)} %copy-done.2, bf16[384,1280]{1,0:T(8,128)(2,1)S(1)} %shard_map.137.refs_4_, ...), custom_call_target="tpu_custom_call" | custom-call | flops 1000 | bytes 1000 | tf_op jit(solution)/shard_map/pallas_call | solution.py:83
  70.3 4.6 %all-to-all-start = ((bf16[4,192,512]{2,1,0:T(8,128)(2,1)}), bf16[4,192,512]{2,1,0:T(8,128)(2,1)S(1)}, u32[]{:S(2)}, u32[]{:S(2)}) async-start(bf16[4,192,512]{2,1,0:T(8,128)(2,1)} %bitcast.6), calls=%async_computation | async-start | bytes 1572864 | tf_op jit(solution)/shard_map/all_to_all | solution.py:36
  75.0 26.1 %all-gather = bf16[256,384]{1,0:T(8,128)(2,1)S(1)} all-gather(bf16[64,384]{1,0:T(8,128)(2,1)S(1)} %shard_map.142), channel_id=2, replica_groups=mesh['x'=4,'zl'=4,'zh'=4,'y'=4,'c'=2] {'zh'}, dimensions={0}, use_global_device_ids=true | all-gather | bytes 245760 | tf_op jit(solution)/shard_map/all_gather | solution.py:274
  102.1 6.7 %all-to-all-start.1 = ((bf16[4,192,512]{2,1,0:T(8,128)(2,1)}), bf16[4,192,512]{2,1,0:T(8,128)(2,1)}, u32[]{:S(2)}, u32[]{:S(2)}) async-start(bf16[4,192,512]{2,1,0:T(8,128)(2,1)} %shard_map.143.refs_9_.refs_1_), calls=%async_computation.1 | async-start | bytes 1572864 | tf_op jit(solution)/shard_map/all_to_all | solution.py:36
  108.9 14.1 %all-gather.1 = bf16[16,64,384]{2,1,0:T(8,128)(2,1)S(1)} all-gather(bf16[4,64,384]{2,1,0:T(8,128)(2,1)S(1)} %shard_map.145), channel_id=3, replica_groups=mesh['x'=4,'zl'=4,'zh'=4,'y'=4,'c'=2] {'y'}, dimensions={0}, use_global_device_ids=true | all-gather | bytes 983040 | tf_op jit(solution)/shard_map/all_gather | solution.py:278
  128.0 17.0 %all-to-all-done.1.refs_0_ = bf16[4,192,512]{2,1,0:T(8,128)(2,1)} async-done(((bf16[4,192,512]{2,1,0:T(8,128)(2,1)}), bf16[4,192,512]{2,1,0:T(8,128)(2,1)}, u32[]{:S(2)}, u32[]{:S(2)}) %all-to-all-start.1) | async-done | bytes 786464 | tf_op jit(solution)/shard_map/all_to_all | solution.py:36
  148.2 8.3 %all-to-all-start.2 = ((bf16[4,192,512]{2,1,0:T(8,128)(2,1)}), bf16[4,192,512]{2,1,0:T(8,128)(2,1)S(1)}, u32[]{:S(2)}, u32[]{:S(2)}) async-start(bf16[4,192,512]{2,1,0:T(8,128)(2,1)} %shard_map.146.refs_3_), calls=%async_computation.2 | async-start | bytes 1572864 | tf_op jit(solution)/shard_map/all_to_all | solution.py:36
  156.6 6.6 %shard_map.147 = (f32[192,924]{1,0:T(8,128)}, f32[192,924]{1,0:T(8,128)}, f32[8,128]{1,0:T(8,128)S(1)}) custom-call(bf16[4,1856,512]{2,1,0:T(8,128)(2,1)} %bitcast.50, bf16[4,4,64,384]{3,2,1,0:T(8,128)(2,1)S(1)} %bitcast.44, bf16[4,4,64,384]{3,2,1,0:T(8,128)(2,1)S(1)} %copy-done.14, bf16[4,192,512]{2,1,0:T(8,128)(2,1)} %shard_map.146.refs_3_), custom_call_target="tpu_custom_call" | custom-call | flops 1000 | bytes 1000 | tf_op jit(solution)/shard_map/pallas_call | solution.py:45
  163.1 2.9 %all-to-all-done.2 = bf16[4,192,512]{2,1,0:T(8,128)(2,1)S(1)} async-done(((bf16[4,192,512]{2,1,0:T(8,128)(2,1)}), bf16[4,192,512]{2,1,0:T(8,128)(2,1)S(1)}, u32[]{:S(2)}, u32[]{:S(2)}) %all-to-all-start.2) | async-done | bytes 786464 | tf_op jit(solution)/shard_map/all_to_all | solution.py:36
  168.0 2.3 %collective-permute-done.9.refs_3_ = bf16[768,512]{1,0:T(8,128)(2,1)S(1)} collective-permute-done((bf16[768,512]{1,0:T(8,128)(2,1)S(1)}, bf16[768,512]{1,0:T(8,128)(2,1)S(1)}, u32[]{:S(2)}, u32[]{:S(2)}) %collective-permute-start.9) | collective-permute-done | bytes 786464 | tf_op jit(solution)/shard_map/ppermute | solution.py:284
  170.3 2.2 %shard_map.149 = (bf16[4,384,256]{2,1,0:T(8,128)(2,1)}, f32[128,256]{1,0:T(8,128)S(1)}, bf16[128,256]{1,0:T(8,128)(2,1)S(1)}, bf16[128,256]{1,0:T(8,128)(2,1)S(1)}, bf16[128,256]{1,0:T(8,128)(2,1)S(1)}) custom-call(bf16[256,512]{1,0:T(8,128)(2,1)S(1)} %get-tuple-element.17.refs_2_.refs_0_, bf16[4,384,256]{2,1,0:T(8,128)(2,1)S(1)} %copy-done.17, ...), custom_call_target="tpu_custom_call" | custom-call | flops 1000 | bytes 1000 | tf_op jit(solution)/shard_map/pallas_call | solution.py:45
  172.5 4.4 %all-to-all-start.3 = ((bf16[4,384,256]{2,1,0:T(8,128)(2,1)}), bf16[4,384,256]{2,1,0:T(8,128)(2,1)S(1)}, u32[]{:S(2)}, u32[]{:S(2)}) async-start(bf16[4,384,256]{2,1,0:T(8,128)(2,1)} %get-tuple-element.20), calls=%async_computation.3 | async-start | bytes 1572864 | tf_op jit(solution)/shard_map/all_to_all | solution.py:36
  178.8 4.6 %collective-permute-start.11 = (bf16[128,256]{1,0:T(8,128)(2,1)S(1)}, bf16[128,256]{1,0:T(8,128)(2,1)S(1)}, u32[]{:S(2)}, u32[]{:S(2)}) collective-permute-start(bf16[128,256]{1,0:T(8,128)(2,1)S(1)} %get-tuple-element.27), channel_id=1, source_target_pairs={{0,96},{64,32},{96,0},{32,64},{1,97},{65,33},{97,1},{33,65},{2,98}... | collective-permute-start | bytes 196616 | tf_op jit(solution)/shard_map/ppermute | solution.py:32
  183.4 3.9 %collective-permute-start.12 = (bf16[128,256]{1,0:T(8,128)(2,1)S(1)}, bf16[128,256]{1,0:T(8,128)(2,1)S(1)}, u32[]{:S(2)}, u32[]{:S(2)}) collective-permute-start(bf16[128,256]{1,0:T(8,128)(2,1)S(1)} %get-tuple-element.28), channel_id=1, source_target_pairs={{0,64},{64,96},{96,32},{32,0},{1,65},{65,97},{97,33},{33,1},{2,66}... | collective-permute-start | bytes 196616 | tf_op jit(solution)/shard_map/ppermute | solution.py:32
  187.4 2.2 %collective-permute-done.12.refs_3_ = bf16[128,256]{1,0:T(8,128)(2,1)S(1)} collective-permute-done((bf16[128,256]{1,0:T(8,128)(2,1)S(1)}, bf16[128,256]{1,0:T(8,128)(2,1)S(1)}, u32[]{:S(2)}, u32[]{:S(2)}) %collective-permute-start.12) | collective-permute-done | bytes 65568 | tf_op jit(solution)/shard_map/ppermute | solution.py:32
  (86 shorter events, 28.2 us)
Async XLA Ops:
  7.2 149.4 %all-gather.5.cloned.1.call-start = ((), (), s32[]{:S(2)}) async-start(), calls=%async_computation.4 | async-start | bytes 9502720 | tf_op jit(solution)/shard_map/all_gather | solution.py:271
  10.0 29.7 %collective-permute-start.3 = (bf16[384,1280]{1,0:T(8,128)(2,1)S(1)}, bf16[384,1280]{1,0:T(8,128)(2,1)S(1)}, u32[]{:S(2)}, u32[]{:S(2)}) collective-permute-start(bf16[384,1280]{1,0:T(8,128)(2,1)S(1)} %shard_map.137.refs_4_), channel_id=1, source_target_pairs={{0,128},{128,256},{256,384},{384,0},{1,129},{129,257},{257,385},{3... | collective-permute-start | bytes 2949128 | tf_op jit(solution)/shard_map/ppermute | solution.py:28
  13.4 29.2 %collective-permute-start.5 = (bf16[384,1280]{1,0:T(8,128)(2,1)S(1)}, bf16[384,1280]{1,0:T(8,128)(2,1)S(1)}, u32[]{:S(2)}, u32[]{:S(2)}) collective-permute-start(bf16[384,1280]{1,0:T(8,128)(2,1)S(1)} %shard_map.137.refs_4_), channel_id=1, source_target_pairs={{0,384},{128,0},{256,128},{384,256},{1,385},{129,1},{257,129},{385... | collective-permute-start | bytes 2949128 | tf_op jit(solution)/shard_map/ppermute | solution.py:28
  19.7 14.7 %collective-permute-start = (bf16[2112,128]{1,0:T(8,128)(2,1)S(1)}, bf16[2112,128]{1,0:T(8,128)(2,1)S(1)}, u32[]{:S(2)}, u32[]{:S(2)}) collective-permute-start(bf16[2112,128]{1,0:T(8,128)(2,1)S(1)} %fusion.4.refs_4_.refs_0_), channel_id=1, source_target_pairs={{0,64},{64,96},{96,32},{32,0},{1,65},{65,97},{97,33},{33,1},{2,66}... | collective-permute-start | bytes 1622024 | tf_op jit(solution)/shard_map/ppermute | solution.py:32
  21.7 25.5 %collective-permute-start.2 = (bf16[2112,128]{1,0:T(8,128)(2,1)S(1)}, bf16[2112,128]{1,0:T(8,128)(2,1)S(1)}, u32[]{:S(2)}, u32[]{:S(2)}) collective-permute-start(bf16[2112,128]{1,0:T(8,128)(2,1)S(1)} %fusion.4.refs_4_.refs_0_), channel_id=1, source_target_pairs={{0,32},{64,0},{96,64},{32,96},{1,33},{65,1},{97,65},{33,97},{2,34}... | collective-permute-start | bytes 1622024 | tf_op jit(solution)/shard_map/ppermute | solution.py:32
  34.4 22.8 %collective-permute-start.1 = (bf16[2112,128]{1,0:T(8,128)(2,1)S(1)}, bf16[2112,128]{1,0:T(8,128)(2,1)S(1)}, u32[]{:S(2)}, u32[]{:S(2)}) collective-permute-start(bf16[2112,128]{1,0:T(8,128)(2,1)S(1)} %collective-permute-done.refs_1_), channel_id=1, source_target_pairs={{0,64},{64,96},{96,32},{32,0},{1,65},{65,97},{97,33},{33,1},{2,66}... | collective-permute-start | bytes 1622024 | tf_op jit(solution)/shard_map/ppermute | solution.py:32
  39.7 24.2 %copy-start = (bf16[384,1280]{1,0:T(8,128)(2,1)}, bf16[384,1280]{1,0:T(8,128)(2,1)S(1)}, u32[]{:S(2)}) copy-start(bf16[384,1280]{1,0:T(8,128)(2,1)S(1)} %collective-permute-done.3.refs_5_) | copy-start | bytes 2949124
  39.8 17.5 %collective-permute-start.4 = (bf16[192,1280]{1,0:T(8,128)(2,1)S(1)}, bf16[192,1280]{1,0:T(8,128)(2,1)S(1)}, u32[]{:S(2)}, u32[]{:S(2)}) collective-permute-start(bf16[192,1280]{1,0:T(8,128)(2,1)S(1)} %slice.8), channel_id=1, source_target_pairs={{0,128},{128,256},{256,384},{384,0},{1,129},{129,257},{257,385},{3... | collective-permute-start | bytes 1474568 | tf_op jit(solution)/shard_map/ppermute | solution.py:28
  42.6 14.7 %copy-start.22 = (bf16[384,1280]{1,0:T(8,128)(2,1)}, bf16[384,1280]{1,0:T(8,128)(2,1)S(1)}, u32[]{:S(2)}) copy-start(bf16[384,1280]{1,0:T(8,128)(2,1)S(1)} %collective-permute-done.5.refs_8_) | copy-start | bytes 2949124
  42.6 14.7 %collective-permute-start.6 = (bf16[192,1280]{1,0:T(8,128)(2,1)S(1)}, bf16[192,1280]{1,0:T(8,128)(2,1)S(1)}, u32[]{:S(2)}, u32[]{:S(2)}) collective-permute-start(bf16[192,1280]{1,0:T(8,128)(2,1)S(1)} %slice.9), channel_id=1, source_target_pairs={{0,384},{128,0},{256,128},{384,256},{1,385},{129,1},{257,129},{385... | collective-permute-start | bytes 1474568 | tf_op jit(solution)/shard_map/ppermute | solution.py:28
  47.2 12.3 %copy-start.1 = (bf16[2112,128]{1,0:T(8,128)(2,1)}, bf16[2112,128]{1,0:T(8,128)(2,1)S(1)}, u32[]{:S(2)}) copy-start(bf16[2112,128]{1,0:T(8,128)(2,1)S(1)} %collective-permute-done.2.refs_3_) | copy-start | bytes 1622020
  62.0 7.3 %collective-permute-start.7 = (bf16[768,512]{1,0:T(8,128)(2,1)}, bf16[768,512]{1,0:T(8,128)(2,1)S(1)}, u32[]{:S(2)}, u32[]{:S(2)}) collective-permute-start(bf16[768,512]{1,0:T(8,128)(2,1)} %copy-done.15), channel_id=1, source_target_pairs={{0,1},{1,0},{2,3},{3,2},{4,5},{5,4},{6,7},{7,6},{8,9},{9,8},{10,11... | collective-permute-start | bytes 2359304 | tf_op jit(solution)/shard_map/ppermute | solution.py:273
  70.3 30.8 %all-to-all-start = ((bf16[4,192,512]{2,1,0:T(8,128)(2,1)}), bf16[4,192,512]{2,1,0:T(8,128)(2,1)S(1)}, u32[]{:S(2)}, u32[]{:S(2)}) async-start(bf16[4,192,512]{2,1,0:T(8,128)(2,1)} %bitcast.6), calls=%async_computation | async-start | bytes 1572864 | tf_op jit(solution)/shard_map/all_to_all | solution.py:36
  102.1 42.8 %all-to-all-start.1 = ((bf16[4,192,512]{2,1,0:T(8,128)(2,1)}), bf16[4,192,512]{2,1,0:T(8,128)(2,1)}, u32[]{:S(2)}, u32[]{:S(2)}) async-start(bf16[4,192,512]{2,1,0:T(8,128)(2,1)} %shard_map.143.refs_9_.refs_1_), calls=%async_computation.1 | async-start | bytes 1572864 | tf_op jit(solution)/shard_map/all_to_all | solution.py:36
  108.8 16.1 %copy-start.3 = (bf16[2112,128]{1,0:T(8,128)(2,1)S(1)}, bf16[2112,128]{1,0:T(8,128)(2,1)}, u32[]{:S(2)}) copy-start(bf16[2112,128]{1,0:T(8,128)(2,1)} %copy-done.1) | copy-start | bytes 1622020
  108.8 16.1 %copy-start.6 = (bf16[2112,128]{1,0:T(8,128)(2,1)S(1)}, bf16[2112,128]{1,0:T(8,128)(2,1)}, u32[]{:S(2)}) copy-start(bf16[2112,128]{1,0:T(8,128)(2,1)} %copy-done.4) | copy-start | bytes 1622020
  108.8 16.1 %copy-start.9 = (bf16[192,1280]{1,0:T(8,128)(2,1)S(1)}, bf16[192,1280]{1,0:T(8,128)(2,1)}, u32[]{:S(2)}) copy-start(bf16[192,1280]{1,0:T(8,128)(2,1)} %copy-done.7) | copy-start | bytes 1474564
  123.0 4.2 %collective-permute-start.8 = (bf16[4,4,64,384]{3,2,1,0:T(8,128)(2,1)S(1)}, bf16[4,4,64,384]{3,2,1,0:T(8,128)(2,1)S(1)}, u32[]{:S(2)}, u32[]{:S(2)}) collective-permute-start(bf16[4,4,64,384]{3,2,1,0:T(8,128)(2,1)S(1)} %bitcast.43), channel_id=1, source_target_pairs={{0,1},{1,0},{2,3},{3,2},{4,5},{5,4},{6,7},{7,6},{8,9},{9,8},{10,11... | collective-permute-start | bytes 2359304 | tf_op jit(solution)/shard_map/ppermute | solution.py:279
  148.2 17.8 %all-to-all-start.2 = ((bf16[4,192,512]{2,1,0:T(8,128)(2,1)}), bf16[4,192,512]{2,1,0:T(8,128)(2,1)S(1)}, u32[]{:S(2)}, u32[]{:S(2)}) async-start(bf16[4,192,512]{2,1,0:T(8,128)(2,1)} %shard_map.146.refs_3_), calls=%async_computation.2 | async-start | bytes 1572864 | tf_op jit(solution)/shard_map/all_to_all | solution.py:36
  166.1 4.2 %collective-permute-start.9 = (bf16[768,512]{1,0:T(8,128)(2,1)S(1)}, bf16[768,512]{1,0:T(8,128)(2,1)S(1)}, u32[]{:S(2)}, u32[]{:S(2)}) collective-permute-start(bf16[768,512]{1,0:T(8,128)(2,1)S(1)} %shard_map.148.refs_2_), channel_id=1, source_target_pairs={{0,1},{1,0},{2,3},{3,2},{4,5},{5,4},{6,7},{7,6},{8,9},{9,8},{10,11... | collective-permute-start | bytes 2359304 | tf_op jit(solution)/shard_map/ppermute | solution.py:284
  172.5 17.8 %all-to-all-start.3 = ((bf16[4,384,256]{2,1,0:T(8,128)(2,1)}), bf16[4,384,256]{2,1,0:T(8,128)(2,1)S(1)}, u32[]{:S(2)}, u32[]{:S(2)}) async-start(bf16[4,384,256]{2,1,0:T(8,128)(2,1)} %get-tuple-element.20), calls=%async_computation.3 | async-start | bytes 1572864 | tf_op jit(solution)/shard_map/all_to_all | solution.py:36
  176.9 10.5 %collective-permute-start.10 = (bf16[128,256]{1,0:T(8,128)(2,1)S(1)}, bf16[128,256]{1,0:T(8,128)(2,1)S(1)}, u32[]{:S(2)}, u32[]{:S(2)}) collective-permute-start(bf16[128,256]{1,0:T(8,128)(2,1)S(1)} %get-tuple-element.26), channel_id=1, source_target_pairs={{0,32},{64,0},{96,64},{32,96},{1,33},{65,1},{97,65},{33,97},{2,34}... | collective-permute-start | bytes 196616 | tf_op jit(solution)/shard_map/ppermute | solution.py:32
  178.8 8.6 %collective-permute-start.11 = (bf16[128,256]{1,0:T(8,128)(2,1)S(1)}, bf16[128,256]{1,0:T(8,128)(2,1)S(1)}, u32[]{:S(2)}, u32[]{:S(2)}) collective-permute-start(bf16[128,256]{1,0:T(8,128)(2,1)S(1)} %get-tuple-element.27), channel_id=1, source_target_pairs={{0,96},{64,32},{96,0},{32,64},{1,97},{65,33},{97,1},{33,65},{2,98}... | collective-permute-start | bytes 196616 | tf_op jit(solution)/shard_map/ppermute | solution.py:32
  183.4 6.2 %collective-permute-start.12 = (bf16[128,256]{1,0:T(8,128)(2,1)S(1)}, bf16[128,256]{1,0:T(8,128)(2,1)S(1)}, u32[]{:S(2)}, u32[]{:S(2)}) collective-permute-start(bf16[128,256]{1,0:T(8,128)(2,1)S(1)} %get-tuple-element.28), channel_id=1, source_target_pairs={{0,64},{64,96},{96,32},{32,0},{1,65},{65,97},{97,33},{33,1},{2,66}... | collective-permute-start | bytes 196616 | tf_op jit(solution)/shard_map/ppermute | solution.py:32
  (19 other events, 54.2 us)
Sparse Core Ops, SparseCore 0:
  62.1 86.9 all-gather.4

commit v4 on v3

--- a/solution.py
+++ b/solution.py
@@ -129,7 +129,11 @@
 
 def join_inner(met, factors, rest):
     def copies(ins, outs, held):
-        pairs = [(ins[k].at[2 * PAD :, :], outs[0].at[:, 128 * k : 128 * (k + 1)]) for k in range(4)]
+        pairs = []
+        for k in range(4):
+            for half in range(2):
+                start, place = 2 * PAD + 128 * half, slice(128 * half, 128 * (half + 1))
+                pairs.append((ins[k].at[start : start + 128, :], outs[0].at[128 * k : 128 * (k + 1), place]))
         columns = slice(WIDE, WIDE + 256)
         for s in range(4):
             for b in range(2):
@@ -137,7 +141,7 @@
                 pairs.append((factor_rows(ins[4:], s, rows, b, columns), outs[1].at[s, rows, :]))
         return pairs
 
-    return copy_call(copies, [(256, 512), (4, 384, 256)], [], [*met, *factors], rest)
+    return copy_call(copies, [(512, 256), (4, 384, 256)], [], [*met, *factors], rest)
 
 
 def add(left, right, rest):
@@ -191,22 +195,37 @@
     return kernel_call(body, [((192, 256), F32)] * 2, [value], rest)
 
 
-def last_sums(inputs, inner, mine, away):
+def first_sums(inputs, inner, mine):
+    def body(ins, outs):
+        me = lax.axis_index("x")
+        rows = pl.ds(pl.multiple_of(lax.axis_index("c") * 192, 16), 192)
+        total = jnp.zeros((512, 256), F32)
+        for s in range(4):
+            grad = ins[2][192 * s : 192 * (s + 1), :]
+            outs[0][(me - s + 4) % 4] = dot(grad, ins[0][...], ((1,), (0,))).astype(BF16)
+            total = total + dot(grad, ins[1][s, rows, :], ((0,), (0,)))
+        outs[1][...] = total
+
+    return kernel_call(body, [((4, 192, 256), BF16), ((512, 256), F32)], [inputs, inner, mine])
+
+
+def last_sums(inputs, inner, away, first, total):
     def body(ins, outs):
         core = lax.axis_index("c")
         me = lax.axis_index("x")
-        total = jnp.zeros((512, 256), F32)
-        for ref, branch in ((ins[2], core), (ins[3], 1 - core)):
-            rows = pl.ds(pl.multiple_of(branch * 192, 16), 192)
-            for s in range(4):
-                grad = ref[192 * s : 192 * (s + 1), :]
-                outs[0][(me - s + 4) % 4, rows, :] = dot(grad, ins[0][...], ((1,), (1,))).astype(BF16)
-                total = total + dot(grad, ins[1][s, rows, :], ((0,), (0,)))
+        here = pl.ds(pl.multiple_of(core * 192, 16), 192)
+        rows = pl.ds(pl.multiple_of((1 - core) * 192, 16), 192)
+        total = ins[4][...]
+        for s in range(4):
+            grad = ins[2][192 * s : 192 * (s + 1), :]
+            outs[0][(me - s + 4) % 4, rows, :] = dot(grad, ins[0][...], ((1,), (0,))).astype(BF16)
+            outs[0][s, here, :] = ins[3][s]
+            total = total + dot(grad, ins[1][s, rows, :], ((0,), (0,)))
         for k in range(4):
             outs[1 + k][...] = total[128 * k : 128 * (k + 1)].astype(outs[1 + k].dtype)
 
     out = [((4, 384, 256), BF16), ((128, 256), F32)] + [((128, 256), BF16)] * 3
-    return kernel_call(body, out, [inputs, inner, mine, away])
+    return kernel_call(body, out, [inputs, inner, away, first, total])
 
 
 def input_total(parts, rest):
@@ -258,7 +277,7 @@
 ):
     gate_grad, up_grad = swiglu_back(gate_pre.T, up_pre.T, hidden_grad.T)
     extra = ((0, PAD - FF), (0, 0))
-    sent = jnp.concatenate((jnp.pad(gate_grad, extra), jnp.pad(up_grad, extra), layer_input.T), axis=0)
+    sent = jnp.concatenate((jnp.pad(gate_grad, extra), jnp.pad(up_grad, extra), *jnp.split(layer_input, 2, axis=1)), axis=0)
     back = turn_z(sent, 1)
     ahead = turn_z(sent, -1)
     met = [sent, back, turn_z(back, 1), ahead]
@@ -278,12 +297,13 @@
     rank = lax.all_gather(after(rank, [mine]), "y")
     rank_other = lax.ppermute(rank, "c", [(0, 1), (1, 0)])
     mine = exchange(mine, "zh")
-    mine = sum_blocks(mine, 4, [], [rank_other, inputs])
+    mine = sum_blocks(mine, 4, [rank_other], [inputs])
     *outer_grads, token = outer_sums(all_grads, rank, rank_other, [mine])
     mine = after(exchange(mine, "y").reshape(768, 512), [token])
     away = lax.ppermute(mine, "c", [(0, 1), (1, 0)])
 
-    inner_grads, *input_parts = last_sums(inputs, inner, mine, away)
+    first, total = first_sums(inputs, inner, mine)
+    inner_grads, *input_parts = last_sums(inputs, inner, away, first, total)
     inner_grads = inner_total(exchange(inner_grads, "x"), [])
     input_grad = input_total([input_parts[0]] + [turn_z(input_parts[s], -s) for s in (1, 2, 3)], [])
     return (inner_grads[0].T, outer_grads[0], inner_grads[1].T, outer_grads[1], input_grad)

time: 199 us -> 199 us (level)
  the two profiles are of different devices: /device:TPU:2 before, /device:TPU:34 now
where the time goes in v4:
time: 199 us; the launch traced here: 198 us
  starting transfers between devices  62.9 us (32%)
  waiting for transfers between devices  49.3 us (25%)
  blocking collectives  39.7 us (20%)
  Pallas kernels  21.8 us (11%)
  between operations  14.5 us (7%)
  local copies, waits for them, and re-layouts  7.81 us (4%)
    ppermute x6, waiting for transfers between devices, turn_z(): lax.ppermute(value, 'zl', [(RING[i], RING[(i + step) % 4]) for i in range...  27.5 us
    all_gather x1, blocking collectives, on_device(): rank = lax.all_gather(after(rank, [mine]), 'zh')  25.4 us
    ppermute x6, starting transfers between devices, turn_z(): lax.ppermute(value, 'zl', [(RING[i], RING[(i + step) % 4]) for i in range...  23.4 us
    all_to_all x4, starting transfers between devices, exchange(): return lax.all_to_all(value, axis, 0, 0)  20.7 us
    all_to_all x4, waiting for transfers between devices, exchange(): return lax.all_to_all(value, axis, 0, 0)  19.8 us
    pallas_call x12, Pallas kernels, kernel_call(): pl.pallas_call(run, out_shape=[jax.ShapeDtypeStruct(shape, dtype) for sha...  14.6 us
    all_gather x1, blocking collectives, on_device(): rank = lax.all_gather(after(rank, [mine]), 'y')  14.3 us
    ppermute x4, starting transfers between devices, turn(): return lax.ppermute(value, axis, [(i, (i + step) % 4) for i in range(4)])  12.9 us
  transfers between devices with their start and end apart: 18, of which 10 were waited for; matrix products, arithmetic and copies ran while one was open for 0% of the time, Pallas kernels for 8%

profile of v4, /device:TPU:34, one launch (start us, length us, event | category | flops | bytes accessed | tf_op | source)
XLA Modules:
  0.0 197.6 jit_solution(1146331805641053210)
XLA Ops:
  9.8 3.4 %collective-permute-start.3 = (bf16[384,1280]{1,0:T(8,128)(2,1)S(1)}, bf16[384,1280]{1,0:T(8,128)(2,1)S(1)}, u32[]{:S(2)}, u32[]{:S(2)}) collective-permute-start(bf16[384,1280]{1,0:T(8,128)(2,1)S(1)} %shard_map.137.refs_4_), channel_id=1, source_target_pairs={{0,128},{128,256},{256,384},{384,0},{1,129},{129,257},{257,385},{3... | collective-permute-start | bytes 2949128 | tf_op jit(solution)/shard_map/ppermute | solution.py:28
  13.2 2.4 %collective-permute-start.5 = (bf16[384,1280]{1,0:T(8,128)(2,1)S(1)}, bf16[384,1280]{1,0:T(8,128)(2,1)S(1)}, u32[]{:S(2)}, u32[]{:S(2)}) collective-permute-start(bf16[384,1280]{1,0:T(8,128)(2,1)S(1)} %shard_map.137.refs_4_), channel_id=1, source_target_pairs={{0,384},{128,0},{256,128},{384,256},{1,385},{129,1},{257,129},{385... | collective-permute-start | bytes 2949128 | tf_op jit(solution)/shard_map/ppermute | solution.py:28
  15.7 5.9 %collective-permute-start = (bf16[2112,128]{1,0:T(8,128)(2,1)S(1)}, bf16[2112,128]{1,0:T(8,128)(2,1)S(1)}, u32[]{:S(2)}, u32[]{:S(2)}) collective-permute-start(bf16[2112,128]{1,0:T(8,128)(2,1)S(1)} %fusion.5.refs_4_.refs_0_), channel_id=1, source_target_pairs={{0,64},{64,96},{96,32},{32,0},{1,65},{65,97},{97,33},{33,1},{2,66}... | collective-permute-start | bytes 1622024 | tf_op jit(solution)/shard_map/ppermute | solution.py:32
  23.5 10.5 %collective-permute-done.refs_1_ = bf16[2112,128]{1,0:T(8,128)(2,1)S(1)} collective-permute-done((bf16[2112,128]{1,0:T(8,128)(2,1)S(1)}, bf16[2112,128]{1,0:T(8,128)(2,1)S(1)}, u32[]{:S(2)}, u32[]{:S(2)}) %collective-permute-start) | collective-permute-done | bytes 540704 | tf_op jit(solution)/shard_map/ppermute | solution.py:32
  34.1 2.2 %collective-permute-start.1 = (bf16[2112,128]{1,0:T(8,128)(2,1)S(1)}, bf16[2112,128]{1,0:T(8,128)(2,1)S(1)}, u32[]{:S(2)}, u32[]{:S(2)}) collective-permute-start(bf16[2112,128]{1,0:T(8,128)(2,1)S(1)} %collective-permute-done.refs_1_), channel_id=1, source_target_pairs={{0,64},{64,96},{96,32},{32,0},{1,65},{65,97},{97,33},{33,1},{2,66}... | collective-permute-start | bytes 1622024 | tf_op jit(solution)/shard_map/ppermute | solution.py:32
  36.3 3.1 %collective-permute-start.4 = (bf16[192,1280]{1,0:T(8,128)(2,1)S(1)}, bf16[192,1280]{1,0:T(8,128)(2,1)S(1)}, u32[]{:S(2)}, u32[]{:S(2)}) collective-permute-start(bf16[192,1280]{1,0:T(8,128)(2,1)S(1)} %slice.8), channel_id=1, source_target_pairs={{0,128},{128,256},{256,384},{384,0},{1,129},{129,257},{257,385},{3... | collective-permute-start | bytes 1474568 | tf_op jit(solution)/shard_map/ppermute | solution.py:28
  39.5 3.9 %collective-permute-start.6 = (bf16[192,1280]{1,0:T(8,128)(2,1)S(1)}, bf16[192,1280]{1,0:T(8,128)(2,1)S(1)}, u32[]{:S(2)}, u32[]{:S(2)}) collective-permute-start(bf16[192,1280]{1,0:T(8,128)(2,1)S(1)} %slice.9), channel_id=1, source_target_pairs={{0,384},{128,0},{256,128},{384,256},{1,385},{129,1},{257,129},{385... | collective-permute-start | bytes 1474568 | tf_op jit(solution)/shard_map/ppermute | solution.py:28
  43.5 2.9 %collective-permute-done.2.refs_3_ = bf16[2112,128]{1,0:T(8,128)(2,1)S(1)} collective-permute-done((bf16[2112,128]{1,0:T(8,128)(2,1)S(1)}, bf16[2112,128]{1,0:T(8,128)(2,1)S(1)}, u32[]{:S(2)}, u32[]{:S(2)}) %collective-permute-start.2) | collective-permute-done | bytes 540704 | tf_op jit(solution)/shard_map/ppermute | solution.py:32
  46.4 9.4 %collective-permute-done.1.refs_2_ = bf16[2112,128]{1,0:T(8,128)(2,1)S(1)} collective-permute-done((bf16[2112,128]{1,0:T(8,128)(2,1)S(1)}, bf16[2112,128]{1,0:T(8,128)(2,1)S(1)}, u32[]{:S(2)}, u32[]{:S(2)}) %collective-permute-start.1) | collective-permute-done | bytes 540704 | tf_op jit(solution)/shard_map/ppermute | solution.py:32
  55.8 2.2 %shard_map.138.refs_4_ = bf16[768,512]{1,0:T(8,128)(2,1)S(1)} custom-call(bf16[2112,128]{1,0:T(8,128)(2,1)S(1)} %fusion.5.refs_4_.refs_0_, bf16[2112,128]{1,0:T(8,128)(2,1)S(1)} %collective-permute-done.refs_1_, bf16[2112,128]{1,0:T(8,128)(2,1)S(1)} %collective-permute-done.1.refs_2_, bf16[2112,128]{1,0:T(8,128)(2,1)S(1)} %collective-permute-done.2.refs_3_, ...), custom_call_target="tpu_custom_call" | custom-call | flops 1000 | bytes 1000 | tf_op jit(solution)/shard_map/pallas_call | solution.py:83
  65.6 2.2 %shard_map.140.refs_0_ = bf16[768,512]{1,0:T(8,128)(2,1)S(1)} custom-call(bf16[2112,128]{1,0:T(8,128)(2,1)S(1)} %fusion.5.refs_4_.refs_0_, bf16[2112,128]{1,0:T(8,128)(2,1)S(1)} %collective-permute-done.refs_1_, bf16[2112,128]{1,0:T(8,128)(2,1)S(1)} %copy-done.5, bf16[2112,128]{1,0:T(8,128)(2,1)S(1)} %copy-done.2, bf16[384,1280]{1,0:T(8,128)(2,1)S(1)} %shard_map.137.refs_4_, ...), custom_call_target="tpu_custom_call" | custom-call | flops 1000 | bytes 1000 | tf_op jit(solution)/shard_map/pallas_call | solution.py:83
  68.9 4.6 %all-to-all-start = ((bf16[4,192,512]{2,1,0:T(8,128)(2,1)}), bf16[4,192,512]{2,1,0:T(8,128)(2,1)S(1)}, u32[]{:S(2)}, u32[]{:S(2)}) async-start(bf16[4,192,512]{2,1,0:T(8,128)(2,1)} %bitcast.5), calls=%async_computation | async-start | bytes 1572864 | tf_op jit(solution)/shard_map/all_to_all | solution.py:36
  73.5 25.4 %all-gather = bf16[256,384]{1,0:T(8,128)(2,1)S(1)} all-gather(bf16[64,384]{1,0:T(8,128)(2,1)S(1)} %shard_map.142), channel_id=2, replica_groups=mesh['x'=4,'zl'=4,'zh'=4,'y'=4,'c'=2] {'zh'}, dimensions={0}, use_global_device_ids=true | all-gather | bytes 245760 | tf_op jit(solution)/shard_map/all_gather | solution.py:293
  99.9 6.6 %all-to-all-start.1 = ((bf16[4,192,512]{2,1,0:T(8,128)(2,1)}), bf16[4,192,512]{2,1,0:T(8,128)(2,1)}, u32[]{:S(2)}, u32[]{:S(2)}) async-start(bf16[4,192,512]{2,1,0:T(8,128)(2,1)} %shard_map.143.refs_9_.refs_1_), calls=%async_computation.1 | async-start | bytes 1572864 | tf_op jit(solution)/shard_map/all_to_all | solution.py:36
  106.6 14.3 %all-gather.1 = bf16[16,64,384]{2,1,0:T(8,128)(2,1)S(1)} all-gather(bf16[4,64,384]{2,1,0:T(8,128)(2,1)S(1)} %shard_map.145), channel_id=3, replica_groups=mesh['x'=4,'zl'=4,'zh'=4,'y'=4,'c'=2] {'y'}, dimensions={0}, use_global_device_ids=true | all-gather | bytes 983040 | tf_op jit(solution)/shard_map/all_gather | solution.py:297
  126.0 14.7 %all-to-all-done.1.refs_0_ = bf16[4,192,512]{2,1,0:T(8,128)(2,1)} async-done(((bf16[4,192,512]{2,1,0:T(8,128)(2,1)}), bf16[4,192,512]{2,1,0:T(8,128)(2,1)}, u32[]{:S(2)}, u32[]{:S(2)}) %all-to-all-start.1) | async-done | bytes 786464 | tf_op jit(solution)/shard_map/all_to_all | solution.py:36
  143.9 4.3 %all-to-all-start.2 = ((bf16[4,192,512]{2,1,0:T(8,128)(2,1)}), bf16[4,192,512]{2,1,0:T(8,128)(2,1)S(1)}, u32[]{:S(2)}, u32[]{:S(2)}) async-start(bf16[4,192,512]{2,1,0:T(8,128)(2,1)} %shard_map.146.refs_3_), calls=%async_computation.2 | async-start | bytes 1572864 | tf_op jit(solution)/shard_map/all_to_all | solution.py:36
  148.6 6.6 %shard_map.147 = (f32[192,924]{1,0:T(8,128)}, f32[192,924]{1,0:T(8,128)}, f32[8,128]{1,0:T(8,128)S(1)}) custom-call(bf16[4,1856,512]{2,1,0:T(8,128)(2,1)} %bitcast.49, bf16[4,4,64,384]{3,2,1,0:T(8,128)(2,1)S(1)} %bitcast.43, bf16[4,4,64,384]{3,2,1,0:T(8,128)(2,1)S(1)} %copy-done.16, bf16[4,192,512]{2,1,0:T(8,128)(2,1)} %shard_map.146.refs_3_), custom_call_target="tpu_custom_call" | custom-call | flops 1000 | bytes 1000 | tf_op jit(solution)/shard_map/pallas_call | solution.py:45
  155.2 5.1 %all-to-all-done.2 = bf16[4,192,512]{2,1,0:T(8,128)(2,1)S(1)} async-done(((bf16[4,192,512]{2,1,0:T(8,128)(2,1)}), bf16[4,192,512]{2,1,0:T(8,128)(2,1)S(1)}, u32[]{:S(2)}, u32[]{:S(2)}) %all-to-all-start.2) | async-done | bytes 786464 | tf_op jit(solution)/shard_map/all_to_all | solution.py:36
  166.0 5.2 %all-to-all-start.3 = ((bf16[4,384,256]{2,1,0:T(8,128)(2,1)}), bf16[4,384,256]{2,1,0:T(8,128)(2,1)S(1)}, u32[]{:S(2)}, u32[]{:S(2)}) async-start(bf16[4,384,256]{2,1,0:T(8,128)(2,1)} %get-tuple-element.24), calls=%async_computation.3 | async-start | bytes 1572864 | tf_op jit(solution)/shard_map/all_to_all | solution.py:36
  171.2 8.1 %collective-permute-start.10 = (bf16[128,256]{1,0:T(8,128)(2,1)S(1)}, bf16[128,256]{1,0:T(8,128)(2,1)S(1)}, u32[]{:S(2)}, u32[]{:S(2)}) collective-permute-start(bf16[128,256]{1,0:T(8,128)(2,1)S(1)} %get-tuple-element.30), channel_id=1, source_target_pairs={{0,32},{64,0},{96,64},{32,96},{1,33},{65,1},{97,65},{33,97},{2,34}... | collective-permute-start | bytes 196616 | tf_op jit(solution)/shard_map/ppermute | solution.py:32
  179.3 2.9 %collective-permute-start.11 = (bf16[128,256]{1,0:T(8,128)(2,1)S(1)}, bf16[128,256]{1,0:T(8,128)(2,1)S(1)}, u32[]{:S(2)}, u32[]{:S(2)}) collective-permute-start(bf16[128,256]{1,0:T(8,128)(2,1)S(1)} %get-tuple-element.31), channel_id=1, source_target_pairs={{0,96},{64,32},{96,0},{32,64},{1,97},{65,33},{97,1},{33,65},{2,98}... | collective-permute-start | bytes 196616 | tf_op jit(solution)/shard_map/ppermute | solution.py:32
  182.2 2.4 %collective-permute-start.12 = (bf16[128,256]{1,0:T(8,128)(2,1)S(1)}, bf16[128,256]{1,0:T(8,128)(2,1)S(1)}, u32[]{:S(2)}, u32[]{:S(2)}) collective-permute-start(bf16[128,256]{1,0:T(8,128)(2,1)S(1)} %get-tuple-element.32), channel_id=1, source_target_pairs={{0,64},{64,96},{96,32},{32,0},{1,65},{65,97},{97,33},{33,1},{2,66}... | collective-permute-start | bytes 196616 | tf_op jit(solution)/shard_map/ppermute | solution.py:32
  186.2 3.1 %collective-permute-done.12.refs_3_ = bf16[128,256]{1,0:T(8,128)(2,1)S(1)} collective-permute-done((bf16[128,256]{1,0:T(8,128)(2,1)S(1)}, bf16[128,256]{1,0:T(8,128)(2,1)S(1)}, u32[]{:S(2)}, u32[]{:S(2)}) %collective-permute-start.12) | collective-permute-done | bytes 65568 | tf_op jit(solution)/shard_map/ppermute | solution.py:32
  (87 shorter events, 31.5 us)
Async XLA Ops:
  7.2 141.4 %all-gather.5.cloned.1.call-start = ((), (), s32[]{:S(2)}) async-start(), calls=%async_computation.4 | async-start | bytes 9502720 | tf_op jit(solution)/shard_map/all_gather | solution.py:290
  9.8 26.4 %collective-permute-start.3 = (bf16[384,1280]{1,0:T(8,128)(2,1)S(1)}, bf16[384,1280]{1,0:T(8,128)(2,1)S(1)}, u32[]{:S(2)}, u32[]{:S(2)}) collective-permute-start(bf16[384,1280]{1,0:T(8,128)(2,1)S(1)} %shard_map.137.refs_4_), channel_id=1, source_target_pairs={{0,128},{128,256},{256,384},{384,0},{1,129},{129,257},{257,385},{3... | collective-permute-start | bytes 2949128 | tf_op jit(solution)/shard_map/ppermute | solution.py:28
  13.2 26.2 %collective-permute-start.5 = (bf16[384,1280]{1,0:T(8,128)(2,1)S(1)}, bf16[384,1280]{1,0:T(8,128)(2,1)S(1)}, u32[]{:S(2)}, u32[]{:S(2)}) collective-permute-start(bf16[384,1280]{1,0:T(8,128)(2,1)S(1)} %shard_map.137.refs_4_), channel_id=1, source_target_pairs={{0,384},{128,0},{256,128},{384,256},{1,385},{129,1},{257,129},{385... | collective-permute-start | bytes 2949128 | tf_op jit(solution)/shard_map/ppermute | solution.py:28
  15.7 18.4 %collective-permute-start = (bf16[2112,128]{1,0:T(8,128)(2,1)S(1)}, bf16[2112,128]{1,0:T(8,128)(2,1)S(1)}, u32[]{:S(2)}, u32[]{:S(2)}) collective-permute-start(bf16[2112,128]{1,0:T(8,128)(2,1)S(1)} %fusion.5.refs_4_.refs_0_), channel_id=1, source_target_pairs={{0,64},{64,96},{96,32},{32,0},{1,65},{65,97},{97,33},{33,1},{2,66}... | collective-permute-start | bytes 1622024 | tf_op jit(solution)/shard_map/ppermute | solution.py:32
  21.6 24.8 %collective-permute-start.2 = (bf16[2112,128]{1,0:T(8,128)(2,1)S(1)}, bf16[2112,128]{1,0:T(8,128)(2,1)S(1)}, u32[]{:S(2)}, u32[]{:S(2)}) collective-permute-start(bf16[2112,128]{1,0:T(8,128)(2,1)S(1)} %fusion.5.refs_4_.refs_0_), channel_id=1, source_target_pairs={{0,32},{64,0},{96,64},{32,96},{1,33},{65,1},{97,65},{33,97},{2,34}... | collective-permute-start | bytes 1622024 | tf_op jit(solution)/shard_map/ppermute | solution.py:32
  34.1 21.7 %collective-permute-start.1 = (bf16[2112,128]{1,0:T(8,128)(2,1)S(1)}, bf16[2112,128]{1,0:T(8,128)(2,1)S(1)}, u32[]{:S(2)}, u32[]{:S(2)}) collective-permute-start(bf16[2112,128]{1,0:T(8,128)(2,1)S(1)} %collective-permute-done.refs_1_), channel_id=1, source_target_pairs={{0,64},{64,96},{96,32},{32,0},{1,65},{65,97},{97,33},{33,1},{2,66}... | collective-permute-start | bytes 1622024 | tf_op jit(solution)/shard_map/ppermute | solution.py:32
  36.3 26.2 %copy-start = (bf16[384,1280]{1,0:T(8,128)(2,1)}, bf16[384,1280]{1,0:T(8,128)(2,1)S(1)}, u32[]{:S(2)}) copy-start(bf16[384,1280]{1,0:T(8,128)(2,1)S(1)} %collective-permute-done.3.refs_5_) | copy-start | bytes 2949124
  36.3 19.5 %collective-permute-start.4 = (bf16[192,1280]{1,0:T(8,128)(2,1)S(1)}, bf16[192,1280]{1,0:T(8,128)(2,1)S(1)}, u32[]{:S(2)}, u32[]{:S(2)}) collective-permute-start(bf16[192,1280]{1,0:T(8,128)(2,1)S(1)} %slice.8), channel_id=1, source_target_pairs={{0,128},{128,256},{256,384},{384,0},{1,129},{129,257},{257,385},{3... | collective-permute-start | bytes 1474568 | tf_op jit(solution)/shard_map/ppermute | solution.py:28
  39.5 16.3 %copy-start.22 = (bf16[384,1280]{1,0:T(8,128)(2,1)}, bf16[384,1280]{1,0:T(8,128)(2,1)S(1)}, u32[]{:S(2)}) copy-start(bf16[384,1280]{1,0:T(8,128)(2,1)S(1)} %collective-permute-done.5.refs_8_) | copy-start | bytes 2949124
  39.5 16.3 %collective-permute-start.6 = (bf16[192,1280]{1,0:T(8,128)(2,1)S(1)}, bf16[192,1280]{1,0:T(8,128)(2,1)S(1)}, u32[]{:S(2)}, u32[]{:S(2)}) collective-permute-start(bf16[192,1280]{1,0:T(8,128)(2,1)S(1)} %slice.9), channel_id=1, source_target_pairs={{0,384},{128,0},{256,128},{384,256},{1,385},{129,1},{257,129},{385... | collective-permute-start | bytes 1474568 | tf_op jit(solution)/shard_map/ppermute | solution.py:28
  46.4 11.7 %copy-start.1 = (bf16[2112,128]{1,0:T(8,128)(2,1)}, bf16[2112,128]{1,0:T(8,128)(2,1)S(1)}, u32[]{:S(2)}) copy-start(bf16[2112,128]{1,0:T(8,128)(2,1)S(1)} %collective-permute-done.2.refs_3_) | copy-start | bytes 1622020
  60.5 7.3 %collective-permute-start.7 = (bf16[768,512]{1,0:T(8,128)(2,1)}, bf16[768,512]{1,0:T(8,128)(2,1)S(1)}, u32[]{:S(2)}, u32[]{:S(2)}) collective-permute-start(bf16[768,512]{1,0:T(8,128)(2,1)} %copy-done.17), channel_id=1, source_target_pairs={{0,1},{1,0},{2,3},{3,2},{4,5},{5,4},{6,7},{7,6},{8,9},{9,8},{10,11... | collective-permute-start | bytes 2359304 | tf_op jit(solution)/shard_map/ppermute | solution.py:292
  68.9 30.1 %all-to-all-start = ((bf16[4,192,512]{2,1,0:T(8,128)(2,1)}), bf16[4,192,512]{2,1,0:T(8,128)(2,1)S(1)}, u32[]{:S(2)}, u32[]{:S(2)}) async-start(bf16[4,192,512]{2,1,0:T(8,128)(2,1)} %bitcast.5), calls=%async_computation | async-start | bytes 1572864 | tf_op jit(solution)/shard_map/all_to_all | solution.py:36
  99.9 40.8 %all-to-all-start.1 = ((bf16[4,192,512]{2,1,0:T(8,128)(2,1)}), bf16[4,192,512]{2,1,0:T(8,128)(2,1)}, u32[]{:S(2)}, u32[]{:S(2)}) async-start(bf16[4,192,512]{2,1,0:T(8,128)(2,1)} %shard_map.143.refs_9_.refs_1_), calls=%async_computation.1 | async-start | bytes 1572864 | tf_op jit(solution)/shard_map/all_to_all | solution.py:36
  106.6 16.3 %copy-start.3 = (bf16[2112,128]{1,0:T(8,128)(2,1)S(1)}, bf16[2112,128]{1,0:T(8,128)(2,1)}, u32[]{:S(2)}) copy-start(bf16[2112,128]{1,0:T(8,128)(2,1)} %copy-done.1) | copy-start | bytes 1622020
  106.6 16.3 %copy-start.6 = (bf16[2112,128]{1,0:T(8,128)(2,1)S(1)}, bf16[2112,128]{1,0:T(8,128)(2,1)}, u32[]{:S(2)}) copy-start(bf16[2112,128]{1,0:T(8,128)(2,1)} %copy-done.4) | copy-start | bytes 1622020
  106.6 16.3 %copy-start.9 = (bf16[192,1280]{1,0:T(8,128)(2,1)S(1)}, bf16[192,1280]{1,0:T(8,128)(2,1)}, u32[]{:S(2)}) copy-start(bf16[192,1280]{1,0:T(8,128)(2,1)} %copy-done.7) | copy-start | bytes 1474564
  120.9 4.2 %collective-permute-start.8 = (bf16[4,4,64,384]{3,2,1,0:T(8,128)(2,1)S(1)}, bf16[4,4,64,384]{3,2,1,0:T(8,128)(2,1)S(1)}, u32[]{:S(2)}, u32[]{:S(2)}) collective-permute-start(bf16[4,4,64,384]{3,2,1,0:T(8,128)(2,1)S(1)} %bitcast.42), channel_id=1, source_target_pairs={{0,1},{1,0},{2,3},{3,2},{4,5},{5,4},{6,7},{7,6},{8,9},{9,8},{10,11... | collective-permute-start | bytes 2359304 | tf_op jit(solution)/shard_map/ppermute | solution.py:298
  143.9 16.3 %all-to-all-start.2 = ((bf16[4,192,512]{2,1,0:T(8,128)(2,1)}), bf16[4,192,512]{2,1,0:T(8,128)(2,1)S(1)}, u32[]{:S(2)}, u32[]{:S(2)}) async-start(bf16[4,192,512]{2,1,0:T(8,128)(2,1)} %shard_map.146.refs_3_), calls=%async_computation.2 | async-start | bytes 1572864 | tf_op jit(solution)/shard_map/all_to_all | solution.py:36
  160.3 4.2 %collective-permute-start.9 = (bf16[768,512]{1,0:T(8,128)(2,1)S(1)}, bf16[768,512]{1,0:T(8,128)(2,1)S(1)}, u32[]{:S(2)}, u32[]{:S(2)}) collective-permute-start(bf16[768,512]{1,0:T(8,128)(2,1)S(1)} %shard_map.148.refs_2_), channel_id=1, source_target_pairs={{0,1},{1,0},{2,3},{3,2},{4,5},{5,4},{6,7},{7,6},{8,9},{9,8},{10,11... | collective-permute-start | bytes 2359304 | tf_op jit(solution)/shard_map/ppermute | solution.py:303
  166.0 23.9 %all-to-all-start.3 = ((bf16[4,384,256]{2,1,0:T(8,128)(2,1)}), bf16[4,384,256]{2,1,0:T(8,128)(2,1)S(1)}, u32[]{:S(2)}, u32[]{:S(2)}) async-start(bf16[4,384,256]{2,1,0:T(8,128)(2,1)} %get-tuple-element.24), calls=%async_computation.3 | async-start | bytes 1572864 | tf_op jit(solution)/shard_map/all_to_all | solution.py:36
  171.2 13.5 %collective-permute-start.10 = (bf16[128,256]{1,0:T(8,128)(2,1)S(1)}, bf16[128,256]{1,0:T(8,128)(2,1)S(1)}, u32[]{:S(2)}, u32[]{:S(2)}) collective-permute-start(bf16[128,256]{1,0:T(8,128)(2,1)S(1)} %get-tuple-element.30), channel_id=1, source_target_pairs={{0,32},{64,0},{96,64},{32,96},{1,33},{65,1},{97,65},{33,97},{2,34}... | collective-permute-start | bytes 196616 | tf_op jit(solution)/shard_map/ppermute | solution.py:32
  179.3 6.9 %collective-permute-start.11 = (bf16[128,256]{1,0:T(8,128)(2,1)S(1)}, bf16[128,256]{1,0:T(8,128)(2,1)S(1)}, u32[]{:S(2)}, u32[]{:S(2)}) collective-permute-start(bf16[128,256]{1,0:T(8,128)(2,1)S(1)} %get-tuple-element.31), channel_id=1, source_target_pairs={{0,96},{64,32},{96,0},{32,64},{1,97},{65,33},{97,1},{33,65},{2,98}... | collective-permute-start | bytes 196616 | tf_op jit(solution)/shard_map/ppermute | solution.py:32
  182.2 7.1 %collective-permute-start.12 = (bf16[128,256]{1,0:T(8,128)(2,1)S(1)}, bf16[128,256]{1,0:T(8,128)(2,1)S(1)}, u32[]{:S(2)}, u32[]{:S(2)}) collective-permute-start(bf16[128,256]{1,0:T(8,128)(2,1)S(1)} %get-tuple-element.32), channel_id=1, source_target_pairs={{0,64},{64,96},{96,32},{32,0},{1,65},{65,97},{97,33},{33,1},{2,66}... | collective-permute-start | bytes 196616 | tf_op jit(solution)/shard_map/ppermute | solution.py:32
  (19 other events, 46.7 us)
Sparse Core Ops, SparseCore 0:
  60.6 87.9 all-gather.4

commit v5 on v4

--- a/solution.py
+++ b/solution.py
@@ -297,7 +297,7 @@
     rank = lax.all_gather(after(rank, [mine]), "y")
     rank_other = lax.ppermute(rank, "c", [(0, 1), (1, 0)])
     mine = exchange(mine, "zh")
-    mine = sum_blocks(mine, 4, [rank_other], [inputs])
+    mine = sum_blocks(mine, 4, [], [inputs])
     *outer_grads, token = outer_sums(all_grads, rank, rank_other, [mine])
     mine = after(exchange(mine, "y").reshape(768, 512), [token])
     away = lax.ppermute(mine, "c", [(0, 1), (1, 0)])

time: 199 us -> 198 us (level)
  local copies, waits for them, and re-layouts: 7.81 us -> 5.81 us
    unnamed x50 -> x40, local copies, waits for them, and re-layouts: 6.96 us -> 4.96 us
  transfers between devices with their start and end apart: 18 -> 18, of which waited for: 10 -> 9; matrix products, arithmetic and copies ran while one was open for 0% -> 0% of each run, Pallas kernels for 8% -> 8%
where the time goes in v5:
time: 198 us; the launch traced here: 196 us
  starting transfers between devices  63.4 us (32%)
  waiting for transfers between devices  48.4 us (24%)
  blocking collectives  40.5 us (20%)
  Pallas kernels  22.2 us (11%)
  between operations  14.4 us (7%)
  local copies, waits for them, and re-layouts  5.81 us (3%)
    ppermute x6, waiting for transfers between devices, turn_z(): lax.ppermute(value, 'zl', [(RING[i], RING[(i + step) % 4]) for i in range...  27.5 us
    all_gather x1, blocking collectives, on_device(): rank = lax.all_gather(after(rank, [mine]), 'zh')  24.9 us
    ppermute x6, starting transfers between devices, turn_z(): lax.ppermute(value, 'zl', [(RING[i], RING[(i + step) % 4]) for i in range...  23.4 us
    all_to_all x4, starting transfers between devices, exchange(): return lax.all_to_all(value, axis, 0, 0)  21.2 us
    all_to_all x4, waiting for transfers between devices, exchange(): return lax.all_to_all(value, axis, 0, 0)  18.6 us
    all_gather x1, blocking collectives, on_device(): rank = lax.all_gather(after(rank, [mine]), 'y')  15.5 us
    pallas_call x12, Pallas kernels, kernel_call(): pl.pallas_call(run, out_shape=[jax.ShapeDtypeStruct(shape, dtype) for sha...  15 us
    ppermute x4, starting transfers between devices, turn(): return lax.ppermute(value, axis, [(i, (i + step) % 4) for i in range(4)])  12.9 us
  transfers between devices with their start and end apart: 18, of which 9 were waited for; matrix products, arithmetic and copies ran while one was open for 0% of the time, Pallas kernels for 8%

profile of v5, /device:TPU:34, one launch (start us, length us, event | category | flops | bytes accessed | tf_op | source)
XLA Modules:
  0.0 196.4 jit_solution(1451399790824935643)
XLA Ops:
  9.8 3.4 %collective-permute-start.3 = (bf16[384,1280]{1,0:T(8,128)(2,1)S(1)}, bf16[384,1280]{1,0:T(8,128)(2,1)S(1)}, u32[]{:S(2)}, u32[]{:S(2)}) collective-permute-start(bf16[384,1280]{1,0:T(8,128)(2,1)S(1)} %shard_map.137.refs_4_), channel_id=1, source_target_pairs={{0,128},{128,256},{256,384},{384,0},{1,129},{129,257},{257,385},{3... | collective-permute-start | bytes 2949128 | tf_op jit(solution)/shard_map/ppermute | solution.py:28
  13.2 2.4 %collective-permute-start.5 = (bf16[384,1280]{1,0:T(8,128)(2,1)S(1)}, bf16[384,1280]{1,0:T(8,128)(2,1)S(1)}, u32[]{:S(2)}, u32[]{:S(2)}) collective-permute-start(bf16[384,1280]{1,0:T(8,128)(2,1)S(1)} %shard_map.137.refs_4_), channel_id=1, source_target_pairs={{0,384},{128,0},{256,128},{384,256},{1,385},{129,1},{257,129},{385... | collective-permute-start | bytes 2949128 | tf_op jit(solution)/shard_map/ppermute | solution.py:28
  15.7 5.9 %collective-permute-start = (bf16[2112,128]{1,0:T(8,128)(2,1)S(1)}, bf16[2112,128]{1,0:T(8,128)(2,1)S(1)}, u32[]{:S(2)}, u32[]{:S(2)}) collective-permute-start(bf16[2112,128]{1,0:T(8,128)(2,1)S(1)} %fusion.5.refs_4_.refs_0_), channel_id=1, source_target_pairs={{0,64},{64,96},{96,32},{32,0},{1,65},{65,97},{97,33},{33,1},{2,66}... | collective-permute-start | bytes 1622024 | tf_op jit(solution)/shard_map/ppermute | solution.py:32
  23.5 10.5 %collective-permute-done.refs_1_ = bf16[2112,128]{1,0:T(8,128)(2,1)S(1)} collective-permute-done((bf16[2112,128]{1,0:T(8,128)(2,1)S(1)}, bf16[2112,128]{1,0:T(8,128)(2,1)S(1)}, u32[]{:S(2)}, u32[]{:S(2)}) %collective-permute-start) | collective-permute-done | bytes 540704 | tf_op jit(solution)/shard_map/ppermute | solution.py:32
  34.1 2.2 %collective-permute-start.1 = (bf16[2112,128]{1,0:T(8,128)(2,1)S(1)}, bf16[2112,128]{1,0:T(8,128)(2,1)S(1)}, u32[]{:S(2)}, u32[]{:S(2)}) collective-permute-start(bf16[2112,128]{1,0:T(8,128)(2,1)S(1)} %collective-permute-done.refs_1_), channel_id=1, source_target_pairs={{0,64},{64,96},{96,32},{32,0},{1,65},{65,97},{97,33},{33,1},{2,66}... | collective-permute-start | bytes 1622024 | tf_op jit(solution)/shard_map/ppermute | solution.py:32
  36.3 3.1 %collective-permute-start.4 = (bf16[192,1280]{1,0:T(8,128)(2,1)S(1)}, bf16[192,1280]{1,0:T(8,128)(2,1)S(1)}, u32[]{:S(2)}, u32[]{:S(2)}) collective-permute-start(bf16[192,1280]{1,0:T(8,128)(2,1)S(1)} %slice.8), channel_id=1, source_target_pairs={{0,128},{128,256},{256,384},{384,0},{1,129},{129,257},{257,385},{3... | collective-permute-start | bytes 1474568 | tf_op jit(solution)/shard_map/ppermute | solution.py:28
  39.5 3.9 %collective-permute-start.6 = (bf16[192,1280]{1,0:T(8,128)(2,1)S(1)}, bf16[192,1280]{1,0:T(8,128)(2,1)S(1)}, u32[]{:S(2)}, u32[]{:S(2)}) collective-permute-start(bf16[192,1280]{1,0:T(8,128)(2,1)S(1)} %slice.9), channel_id=1, source_target_pairs={{0,384},{128,0},{256,128},{384,256},{1,385},{129,1},{257,129},{385... | collective-permute-start | bytes 1474568 | tf_op jit(solution)/shard_map/ppermute | solution.py:28
  43.5 2.9 %collective-permute-done.2.refs_3_ = bf16[2112,128]{1,0:T(8,128)(2,1)S(1)} collective-permute-done((bf16[2112,128]{1,0:T(8,128)(2,1)S(1)}, bf16[2112,128]{1,0:T(8,128)(2,1)S(1)}, u32[]{:S(2)}, u32[]{:S(2)}) %collective-permute-start.2) | collective-permute-done | bytes 540704 | tf_op jit(solution)/shard_map/ppermute | solution.py:32
  46.4 9.4 %collective-permute-done.1.refs_2_ = bf16[2112,128]{1,0:T(8,128)(2,1)S(1)} collective-permute-done((bf16[2112,128]{1,0:T(8,128)(2,1)S(1)}, bf16[2112,128]{1,0:T(8,128)(2,1)S(1)}, u32[]{:S(2)}, u32[]{:S(2)}) %collective-permute-start.1) | collective-permute-done | bytes 540704 | tf_op jit(solution)/shard_map/ppermute | solution.py:32
  55.8 2.2 %shard_map.138.refs_4_ = bf16[768,512]{1,0:T(8,128)(2,1)S(1)} custom-call(bf16[2112,128]{1,0:T(8,128)(2,1)S(1)} %fusion.5.refs_4_.refs_0_, bf16[2112,128]{1,0:T(8,128)(2,1)S(1)} %collective-permute-done.refs_1_, bf16[2112,128]{1,0:T(8,128)(2,1)S(1)} %collective-permute-done.1.refs_2_, bf16[2112,128]{1,0:T(8,128)(2,1)S(1)} %collective-permute-done.2.refs_3_, ...), custom_call_target="tpu_custom_call" | custom-call | flops 1000 | bytes 1000 | tf_op jit(solution)/shard_map/pallas_call | solution.py:83
  65.6 2.2 %shard_map.140.refs_0_ = bf16[768,512]{1,0:T(8,128)(2,1)S(1)} custom-call(bf16[2112,128]{1,0:T(8,128)(2,1)S(1)} %fusion.5.refs_4_.refs_0_, bf16[2112,128]{1,0:T(8,128)(2,1)S(1)} %collective-permute-done.refs_1_, bf16[2112,128]{1,0:T(8,128)(2,1)S(1)} %copy-done.5, bf16[2112,128]{1,0:T(8,128)(2,1)S(1)} %copy-done.2, bf16[384,1280]{1,0:T(8,128)(2,1)S(1)} %shard_map.137.refs_4_, ...), custom_call_target="tpu_custom_call" | custom-call | flops 1000 | bytes 1000 | tf_op jit(solution)/shard_map/pallas_call | solution.py:83
  68.9 4.6 %all-to-all-start = ((bf16[4,192,512]{2,1,0:T(8,128)(2,1)}), bf16[4,192,512]{2,1,0:T(8,128)(2,1)S(1)}, u32[]{:S(2)}, u32[]{:S(2)}) async-start(bf16[4,192,512]{2,1,0:T(8,128)(2,1)} %bitcast.5), calls=%async_computation | async-start | bytes 1572864 | tf_op jit(solution)/shard_map/all_to_all | solution.py:36
  73.5 24.9 %all-gather = bf16[256,384]{1,0:T(8,128)(2,1)S(1)} all-gather(bf16[64,384]{1,0:T(8,128)(2,1)S(1)} %shard_map.142), channel_id=2, replica_groups=mesh['x'=4,'zl'=4,'zh'=4,'y'=4,'c'=2] {'zh'}, dimensions={0}, use_global_device_ids=true | all-gather | bytes 245760 | tf_op jit(solution)/shard_map/all_gather | solution.py:293
  99.5 6.6 %all-to-all-start.1 = ((bf16[4,192,512]{2,1,0:T(8,128)(2,1)}), bf16[4,192,512]{2,1,0:T(8,128)(2,1)}, u32[]{:S(2)}, u32[]{:S(2)}) async-start(bf16[4,192,512]{2,1,0:T(8,128)(2,1)} %shard_map.143.refs_9_.refs_1_), calls=%async_computation.1 | async-start | bytes 1572864 | tf_op jit(solution)/shard_map/all_to_all | solution.py:36
  106.1 15.5 %all-gather.2 = bf16[16,64,384]{2,1,0:T(8,128)(2,1)} all-gather(bf16[4,64,384]{2,1,0:T(8,128)(2,1)S(1)} %shard_map.146), channel_id=4, replica_groups=mesh['x'=4,'zl'=4,'zh'=4,'y'=4,'c'=2] {'y'}, dimensions={0}, use_global_device_ids=true | all-gather | bytes 983040 | tf_op jit(solution)/shard_map/all_gather | solution.py:297
  125.8 14.9 %all-to-all-done.1.refs_0_ = bf16[4,192,512]{2,1,0:T(8,128)(2,1)} async-done(((bf16[4,192,512]{2,1,0:T(8,128)(2,1)}), bf16[4,192,512]{2,1,0:T(8,128)(2,1)}, u32[]{:S(2)}, u32[]{:S(2)}) %all-to-all-start.1) | async-done | bytes 786464 | tf_op jit(solution)/shard_map/all_to_all | solution.py:36
  142.8 5.1 %all-to-all-start.2 = ((bf16[4,192,512]{2,1,0:T(8,128)(2,1)}), bf16[4,192,512]{2,1,0:T(8,128)(2,1)S(1)}, u32[]{:S(2)}, u32[]{:S(2)}) async-start(bf16[4,192,512]{2,1,0:T(8,128)(2,1)} %shard_map.145.refs_3_), calls=%async_computation.2 | async-start | bytes 1572864 | tf_op jit(solution)/shard_map/all_to_all | solution.py:36
  148.6 7.0 %shard_map.147 = (f32[192,924]{1,0:T(8,128)}, f32[192,924]{1,0:T(8,128)}, f32[8,128]{1,0:T(8,128)S(1)}) custom-call(bf16[4,1856,512]{2,1,0:T(8,128)(2,1)} %bitcast.47, bf16[4,4,64,384]{3,2,1,0:T(8,128)(2,1)} %bitcast.9.refs_1_, bf16[4,4,64,384]{3,2,1,0:T(8,128)(2,1)} %collective-permute-done.8.refs_2_, bf16[4,192,512]{2,1,0:T(8,128)(2,1)} %shard_map.145.refs_3_), custom_call_target="tpu_custom_call" | custom-call | flops 1000 | bytes 1000 | tf_op jit(solution)/shard_map/pallas_call | solution.py:45
  155.6 3.7 %all-to-all-done.2 = bf16[4,192,512]{2,1,0:T(8,128)(2,1)S(1)} async-done(((bf16[4,192,512]{2,1,0:T(8,128)(2,1)}), bf16[4,192,512]{2,1,0:T(8,128)(2,1)S(1)}, u32[]{:S(2)}, u32[]{:S(2)}) %all-to-all-start.2) | async-done | bytes 786464 | tf_op jit(solution)/shard_map/all_to_all | solution.py:36
  165.1 4.9 %all-to-all-start.3 = ((bf16[4,384,256]{2,1,0:T(8,128)(2,1)}), bf16[4,384,256]{2,1,0:T(8,128)(2,1)S(1)}, u32[]{:S(2)}, u32[]{:S(2)}) async-start(bf16[4,384,256]{2,1,0:T(8,128)(2,1)} %get-tuple-element.24), calls=%async_computation.3 | async-start | bytes 1572864 | tf_op jit(solution)/shard_map/all_to_all | solution.py:36
  170.0 8.1 %collective-permute-start.10 = (bf16[128,256]{1,0:T(8,128)(2,1)S(1)}, bf16[128,256]{1,0:T(8,128)(2,1)S(1)}, u32[]{:S(2)}, u32[]{:S(2)}) collective-permute-start(bf16[128,256]{1,0:T(8,128)(2,1)S(1)} %get-tuple-element.30), channel_id=1, source_target_pairs={{0,32},{64,0},{96,64},{32,96},{1,33},{65,1},{97,65},{33,97},{2,34}... | collective-permute-start | bytes 196616 | tf_op jit(solution)/shard_map/ppermute | solution.py:32
  178.1 2.9 %collective-permute-start.11 = (bf16[128,256]{1,0:T(8,128)(2,1)S(1)}, bf16[128,256]{1,0:T(8,128)(2,1)S(1)}, u32[]{:S(2)}, u32[]{:S(2)}) collective-permute-start(bf16[128,256]{1,0:T(8,128)(2,1)S(1)} %get-tuple-element.31), channel_id=1, source_target_pairs={{0,96},{64,32},{96,0},{32,64},{1,97},{65,33},{97,1},{33,65},{2,98}... | collective-permute-start | bytes 196616 | tf_op jit(solution)/shard_map/ppermute | solution.py:32
  181.0 2.4 %collective-permute-start.12 = (bf16[128,256]{1,0:T(8,128)(2,1)S(1)}, bf16[128,256]{1,0:T(8,128)(2,1)S(1)}, u32[]{:S(2)}, u32[]{:S(2)}) collective-permute-start(bf16[128,256]{1,0:T(8,128)(2,1)S(1)} %get-tuple-element.32), channel_id=1, source_target_pairs={{0,64},{64,96},{96,32},{32,0},{1,65},{65,97},{97,33},{33,1},{2,66}... | collective-permute-start | bytes 196616 | tf_op jit(solution)/shard_map/ppermute | solution.py:32
  185.0 3.1 %collective-permute-done.12.refs_3_ = bf16[128,256]{1,0:T(8,128)(2,1)S(1)} collective-permute-done((bf16[128,256]{1,0:T(8,128)(2,1)S(1)}, bf16[128,256]{1,0:T(8,128)(2,1)S(1)}, u32[]{:S(2)}, u32[]{:S(2)}) %collective-permute-start.12) | collective-permute-done | bytes 65568 | tf_op jit(solution)/shard_map/ppermute | solution.py:32
  (77 shorter events, 29.9 us)
Async XLA Ops:
  7.2 141.4 %all-gather.5.cloned.1.call-start = ((), (), s32[]{:S(2)}) async-start(), calls=%async_computation.4 | async-start | bytes 9502720 | tf_op jit(solution)/shard_map/all_gather | solution.py:290
  9.8 26.4 %collective-permute-start.3 = (bf16[384,1280]{1,0:T(8,128)(2,1)S(1)}, bf16[384,1280]{1,0:T(8,128)(2,1)S(1)}, u32[]{:S(2)}, u32[]{:S(2)}) collective-permute-start(bf16[384,1280]{1,0:T(8,128)(2,1)S(1)} %shard_map.137.refs_4_), channel_id=1, source_target_pairs={{0,128},{128,256},{256,384},{384,0},{1,129},{129,257},{257,385},{3... | collective-permute-start | bytes 2949128 | tf_op jit(solution)/shard_map/ppermute | solution.py:28
  13.2 26.2 %collective-permute-start.5 = (bf16[384,1280]{1,0:T(8,128)(2,1)S(1)}, bf16[384,1280]{1,0:T(8,128)(2,1)S(1)}, u32[]{:S(2)}, u32[]{:S(2)}) collective-permute-start(bf16[384,1280]{1,0:T(8,128)(2,1)S(1)} %shard_map.137.refs_4_), channel_id=1, source_target_pairs={{0,384},{128,0},{256,128},{384,256},{1,385},{129,1},{257,129},{385... | collective-permute-start | bytes 2949128 | tf_op jit(solution)/shard_map/ppermute | solution.py:28
  15.7 18.4 %collective-permute-start = (bf16[2112,128]{1,0:T(8,128)(2,1)S(1)}, bf16[2112,128]{1,0:T(8,128)(2,1)S(1)}, u32[]{:S(2)}, u32[]{:S(2)}) collective-permute-start(bf16[2112,128]{1,0:T(8,128)(2,1)S(1)} %fusion.5.refs_4_.refs_0_), channel_id=1, source_target_pairs={{0,64},{64,96},{96,32},{32,0},{1,65},{65,97},{97,33},{33,1},{2,66}... | collective-permute-start | bytes 1622024 | tf_op jit(solution)/shard_map/ppermute | solution.py:32
  21.6 24.8 %collective-permute-start.2 = (bf16[2112,128]{1,0:T(8,128)(2,1)S(1)}, bf16[2112,128]{1,0:T(8,128)(2,1)S(1)}, u32[]{:S(2)}, u32[]{:S(2)}) collective-permute-start(bf16[2112,128]{1,0:T(8,128)(2,1)S(1)} %fusion.5.refs_4_.refs_0_), channel_id=1, source_target_pairs={{0,32},{64,0},{96,64},{32,96},{1,33},{65,1},{97,65},{33,97},{2,34}... | collective-permute-start | bytes 1622024 | tf_op jit(solution)/shard_map/ppermute | solution.py:32
  34.1 21.7 %collective-permute-start.1 = (bf16[2112,128]{1,0:T(8,128)(2,1)S(1)}, bf16[2112,128]{1,0:T(8,128)(2,1)S(1)}, u32[]{:S(2)}, u32[]{:S(2)}) collective-permute-start(bf16[2112,128]{1,0:T(8,128)(2,1)S(1)} %collective-permute-done.refs_1_), channel_id=1, source_target_pairs={{0,64},{64,96},{96,32},{32,0},{1,65},{65,97},{97,33},{33,1},{2,66}... | collective-permute-start | bytes 1622024 | tf_op jit(solution)/shard_map/ppermute | solution.py:32
  36.3 26.2 %copy-start = (bf16[384,1280]{1,0:T(8,128)(2,1)}, bf16[384,1280]{1,0:T(8,128)(2,1)S(1)}, u32[]{:S(2)}) copy-start(bf16[384,1280]{1,0:T(8,128)(2,1)S(1)} %collective-permute-done.3.refs_5_) | copy-start | bytes 2949124
  36.3 19.5 %collective-permute-start.4 = (bf16[192,1280]{1,0:T(8,128)(2,1)S(1)}, bf16[192,1280]{1,0:T(8,128)(2,1)S(1)}, u32[]{:S(2)}, u32[]{:S(2)}) collective-permute-start(bf16[192,1280]{1,0:T(8,128)(2,1)S(1)} %slice.8), channel_id=1, source_target_pairs={{0,128},{128,256},{256,384},{384,0},{1,129},{129,257},{257,385},{3... | collective-permute-start | bytes 1474568 | tf_op jit(solution)/shard_map/ppermute | solution.py:28
  39.5 16.3 %copy-start.17 = (bf16[384,1280]{1,0:T(8,128)(2,1)}, bf16[384,1280]{1,0:T(8,128)(2,1)S(1)}, u32[]{:S(2)}) copy-start(bf16[384,1280]{1,0:T(8,128)(2,1)S(1)} %collective-permute-done.5.refs_8_) | copy-start | bytes 2949124
  39.5 16.3 %collective-permute-start.6 = (bf16[192,1280]{1,0:T(8,128)(2,1)S(1)}, bf16[192,1280]{1,0:T(8,128)(2,1)S(1)}, u32[]{:S(2)}, u32[]{:S(2)}) collective-permute-start(bf16[192,1280]{1,0:T(8,128)(2,1)S(1)} %slice.9), channel_id=1, source_target_pairs={{0,384},{128,0},{256,128},{384,256},{1,385},{129,1},{257,129},{385... | collective-permute-start | bytes 1474568 | tf_op jit(solution)/shard_map/ppermute | solution.py:28
  46.4 11.7 %copy-start.1 = (bf16[2112,128]{1,0:T(8,128)(2,1)}, bf16[2112,128]{1,0:T(8,128)(2,1)S(1)}, u32[]{:S(2)}) copy-start(bf16[2112,128]{1,0:T(8,128)(2,1)S(1)} %collective-permute-done.2.refs_3_) | copy-start | bytes 1622020
  60.5 7.3 %collective-permute-start.7 = (bf16[768,512]{1,0:T(8,128)(2,1)}, bf16[768,512]{1,0:T(8,128)(2,1)S(1)}, u32[]{:S(2)}, u32[]{:S(2)}) collective-permute-start(bf16[768,512]{1,0:T(8,128)(2,1)} %copy-done.12), channel_id=1, source_target_pairs={{0,1},{1,0},{2,3},{3,2},{4,5},{5,4},{6,7},{7,6},{8,9},{9,8},{10,11... | collective-permute-start | bytes 2359304 | tf_op jit(solution)/shard_map/ppermute | solution.py:292
  68.9 29.6 %all-to-all-start = ((bf16[4,192,512]{2,1,0:T(8,128)(2,1)}), bf16[4,192,512]{2,1,0:T(8,128)(2,1)S(1)}, u32[]{:S(2)}, u32[]{:S(2)}) async-start(bf16[4,192,512]{2,1,0:T(8,128)(2,1)} %bitcast.5), calls=%async_computation | async-start | bytes 1572864 | tf_op jit(solution)/shard_map/all_to_all | solution.py:36
  99.5 41.2 %all-to-all-start.1 = ((bf16[4,192,512]{2,1,0:T(8,128)(2,1)}), bf16[4,192,512]{2,1,0:T(8,128)(2,1)}, u32[]{:S(2)}, u32[]{:S(2)}) async-start(bf16[4,192,512]{2,1,0:T(8,128)(2,1)} %shard_map.143.refs_9_.refs_1_), calls=%async_computation.1 | async-start | bytes 1572864 | tf_op jit(solution)/shard_map/all_to_all | solution.py:36
  106.1 17.5 %copy-start.3 = (bf16[2112,128]{1,0:T(8,128)(2,1)S(1)}, bf16[2112,128]{1,0:T(8,128)(2,1)}, u32[]{:S(2)}) copy-start(bf16[2112,128]{1,0:T(8,128)(2,1)} %copy-done.1) | copy-start | bytes 1622020
  106.1 17.5 %copy-start.6 = (bf16[2112,128]{1,0:T(8,128)(2,1)S(1)}, bf16[2112,128]{1,0:T(8,128)(2,1)}, u32[]{:S(2)}) copy-start(bf16[2112,128]{1,0:T(8,128)(2,1)} %copy-done.4) | copy-start | bytes 1622020
  106.1 17.5 %copy-start.9 = (bf16[192,1280]{1,0:T(8,128)(2,1)S(1)}, bf16[192,1280]{1,0:T(8,128)(2,1)}, u32[]{:S(2)}) copy-start(bf16[192,1280]{1,0:T(8,128)(2,1)} %copy-done.7) | copy-start | bytes 1474564
  121.7 26.3 %collective-permute-start.8 = (bf16[4,4,64,384]{3,2,1,0:T(8,128)(2,1)}, bf16[4,4,64,384]{3,2,1,0:T(8,128)(2,1)}, u32[]{:S(2)}, u32[]{:S(2)}) collective-permute-start(bf16[4,4,64,384]{3,2,1,0:T(8,128)(2,1)} %bitcast.9.refs_1_), channel_id=1, source_target_pairs={{0,1},{1,0},{2,3},{3,2},{4,5},{5,4},{6,7},{7,6},{8,9},{9,8},{10,11... | collective-permute-start | bytes 2359304 | tf_op jit(solution)/shard_map/ppermute | solution.py:298
  142.8 16.5 %all-to-all-start.2 = ((bf16[4,192,512]{2,1,0:T(8,128)(2,1)}), bf16[4,192,512]{2,1,0:T(8,128)(2,1)S(1)}, u32[]{:S(2)}, u32[]{:S(2)}) async-start(bf16[4,192,512]{2,1,0:T(8,128)(2,1)} %shard_map.145.refs_3_), calls=%async_computation.2 | async-start | bytes 1572864 | tf_op jit(solution)/shard_map/all_to_all | solution.py:36
  159.3 4.2 %collective-permute-start.9 = (bf16[768,512]{1,0:T(8,128)(2,1)S(1)}, bf16[768,512]{1,0:T(8,128)(2,1)S(1)}, u32[]{:S(2)}, u32[]{:S(2)}) collective-permute-start(bf16[768,512]{1,0:T(8,128)(2,1)S(1)} %shard_map.148.refs_2_), channel_id=1, source_target_pairs={{0,1},{1,0},{2,3},{3,2},{4,5},{5,4},{6,7},{7,6},{8,9},{9,8},{10,11... | collective-permute-start | bytes 2359304 | tf_op jit(solution)/shard_map/ppermute | solution.py:303
  165.1 23.6 %all-to-all-start.3 = ((bf16[4,384,256]{2,1,0:T(8,128)(2,1)}), bf16[4,384,256]{2,1,0:T(8,128)(2,1)S(1)}, u32[]{:S(2)}, u32[]{:S(2)}) async-start(bf16[4,384,256]{2,1,0:T(8,128)(2,1)} %get-tuple-element.24), calls=%async_computation.3 | async-start | bytes 1572864 | tf_op jit(solution)/shard_map/all_to_all | solution.py:36
  170.0 13.4 %collective-permute-start.10 = (bf16[128,256]{1,0:T(8,128)(2,1)S(1)}, bf16[128,256]{1,0:T(8,128)(2,1)S(1)}, u32[]{:S(2)}, u32[]{:S(2)}) collective-permute-start(bf16[128,256]{1,0:T(8,128)(2,1)S(1)} %get-tuple-element.30), channel_id=1, source_target_pairs={{0,32},{64,0},{96,64},{32,96},{1,33},{65,1},{97,65},{33,97},{2,34}... | collective-permute-start | bytes 196616 | tf_op jit(solution)/shard_map/ppermute | solution.py:32
  178.1 6.9 %collective-permute-start.11 = (bf16[128,256]{1,0:T(8,128)(2,1)S(1)}, bf16[128,256]{1,0:T(8,128)(2,1)S(1)}, u32[]{:S(2)}, u32[]{:S(2)}) collective-permute-start(bf16[128,256]{1,0:T(8,128)(2,1)S(1)} %get-tuple-element.31), channel_id=1, source_target_pairs={{0,96},{64,32},{96,0},{32,64},{1,97},{65,33},{97,1},{33,65},{2,98}... | collective-permute-start | bytes 196616 | tf_op jit(solution)/shard_map/ppermute | solution.py:32
  181.0 7.1 %collective-permute-start.12 = (bf16[128,256]{1,0:T(8,128)(2,1)S(1)}, bf16[128,256]{1,0:T(8,128)(2,1)S(1)}, u32[]{:S(2)}, u32[]{:S(2)}) collective-permute-start(bf16[128,256]{1,0:T(8,128)(2,1)S(1)} %get-tuple-element.32), channel_id=1, source_target_pairs={{0,64},{64,96},{96,32},{32,0},{1,65},{65,97},{97,33},{33,1},{2,66}... | collective-permute-start | bytes 196616 | tf_op jit(solution)/shard_map/ppermute | solution.py:32
  (14 other events, 30.8 us)
Sparse Core Ops, SparseCore 0:
  60.6 87.9 all-gather.4
